TPU v7x, 32 devices: a whole 2x2x4 slice. The times are simulated.
32 devices in a mesh: dp: 16 (over z, y, core), tp: 2 (over x).
Axes of the slice: x: 2, y: 2, z: 4, core: 2. Of those that a mesh axis runs over, the one named last changes fastest.
Arguments:
- tokens: bfloat16 [17408, 768], P('dp'), may hold values from -6 to 6
- latents: bfloat16 [17408, 1024], P('dp'), may hold values from -6 to 6
- grad_block: bfloat16 [17408, 768], P('dp'), may hold values from -6 to 6
- grad_head: bfloat16 [17408, 1024], P('dp'), may hold values from -6 to 6
- image_lengths: int32 [16, 3], P('dp'), may hold values from 0 to 1088, as said below
- ln1_gain: float32 [768], replicated, may hold values from 0.5 to 1.5
- ln1_bias: float32 [768], replicated, may hold values from -1.8 to 1.8
- w_qkv: bfloat16 [3, 768, 768], P(None, 'dp', 'tp'), may hold values from -0.21875 to 0.21875
- b_qv: float32 [2, 768], P(None, 'tp'), may hold values from -1.8 to 1.8
- w_out: bfloat16 [768, 768], P('dp', 'tp'), may hold values from -1.75 to 1.75
- b_out: float32 [768], replicated, may hold values from -1.8 to 1.8
- ln2_gain: float32 [768], replicated, may hold values from 0.5 to 1.5
- ln2_bias: float32 [768], replicated, may hold values from -1.8 to 1.8
- w_up: bfloat16 [768, 3072], P('dp', 'tp'), may hold values from -0.21875 to 0.21875
- b_up: float32 [3072], P('tp'), may hold values from -1.8 to 1.8
- w_down: bfloat16 [768, 3072], P('dp', 'tp'), may hold values from -0.109375 to 0.109375
- b_down: float32 [768], replicated, may hold values from -1.8 to 1.8
- w_mod: bfloat16 [3, 768, 1024], P(None, 'dp'), may hold values from -0.21875 to 0.21875
- b_mod: float32 [3, 1024], replicated, may hold values from -1.8 to 1.8
- w_hid1: bfloat16 [1024, 1024], P('dp', 'tp'), may hold values from -0.1875 to 0.1875
- b_hid1: float32 [1024], P('tp'), may hold values from -1.8 to 1.8
- w_hid2: bfloat16 [1024, 1024], P('dp', 'tp'), may hold values from -0.1875 to 0.1875
- b_hid2: float32 [1024], replicated, may hold values from -1.8 to 1.8
Outputs:
- block_out: bfloat16 [17408, 768], P('dp')
- head_out: bfloat16 [17408, 1024], P('dp')
- grad_tokens: float32 [17408, 768], P('dp')
- grad_latents: float32 [17408, 1024], P('dp')
- d_ln1_gain: float32 [768], replicated
- d_ln1_bias: float32 [768], replicated
- d_w_qkv: float32 [3, 768, 768], P(None, 'dp', 'tp')
- d_b_qv: float32 [2, 768], P(None, 'tp')
- d_w_out: float32 [768, 768], P('dp', 'tp')
- d_b_out: float32 [768], replicated
- d_ln2_gain: float32 [768], replicated
- d_ln2_bias: float32 [768], replicated
- d_w_up: float32 [768, 3072], P('dp', 'tp')
- d_b_up: float32 [3072], P('tp')
- d_w_down: float32 [768, 3072], P('dp', 'tp')
- d_b_down: float32 [768], replicated
- d_w_mod: float32 [3, 768, 1024], P(None, 'dp')
- d_b_mod: float32 [3, 1024], replicated
- d_w_hid1: float32 [1024, 1024], P('dp', 'tp')
- d_b_hid1: float32 [1024], P('tp')
- d_w_hid2: float32 [1024, 1024], P('dp', 'tp')
- d_b_hid2: float32 [1024], replicated
- rms_values: float32 [16, 4], P('dp')
Inputs may be any that keep to these rules, and one draw needn't show every extreme that they name: `image_lengths`: each row describes one slot: either one image of 1088 tokens followed by two zeros, or three images of 320 tokens each, the slot's remaining rows being padding. Both kinds of row occur in every draw.
All inputs are finite; a program needn't handle non-finite values.
Results may differ from a plain program's by a relative error of at most 0.03.
Values may be sent and summed in bfloat16 or wider, within the bound.
No kernel may reach another device: no remote copies, remote signals or barrier semaphores. Data moves between devices by JAX's collectives and lax.ppermute only.
A program may use at most 256 MiB of HBM per device.

v0:
```python
import jax
import jax.numpy as jnp
from jax import lax
from jax.sharding import PartitionSpec as P

HDIM = 64
BUF = 64
LONG = 1024


EPS_NORM = 1e-06
NEG_FILL = -1e30


def norm_parts(values):
    row_mean = jnp.mean(values, axis=-1, keepdims=True)
    centred = values - row_mean
    inv_dev = lax.rsqrt(jnp.mean(centred * centred, axis=-1, keepdims=True) + EPS_NORM)
    return (centred * inv_dev, inv_dev)


def norm_back(grad_norm, normed, inv_dev):
    mean_grad = jnp.mean(grad_norm, axis=-1, keepdims=True)
    mean_cross = jnp.mean(grad_norm * normed, axis=-1, keepdims=True)
    return inv_dev * (grad_norm - mean_grad - normed * mean_cross)


def contract(left, right, left_dim, right_dim):
    return lax.dot_general(
        left, right, (((left_dim,), (right_dim,)), ((), ())), preferred_element_type=jnp.float32
    )


def slot_masks(lengths):
    bounds = jnp.cumsum(lengths)
    positions = jnp.arange(LONG + BUF, dtype=jnp.int32)
    segment = jnp.sum((positions[:, None] >= bounds[None, :]).astype(jnp.int32), axis=1)
    starts = jnp.concatenate([jnp.zeros((1,), jnp.int32), bounds])
    first_row = jnp.sum(
        jnp.where(segment[:, None] == jnp.arange(4, dtype=jnp.int32)[None, :], starts[None, :], 0),
        axis=1,
    )
    valid_row = positions < bounds[2]
    image_row = valid_row & (positions - first_row >= BUF)
    return (segment, valid_row.astype(jnp.float32), image_row.astype(jnp.float32))


def head_forward(q_head, k_head, v_head, same_seg):
    scores = contract(q_head, k_head, 1, 1) * HDIM ** (-0.5)
    scores = jnp.where(same_seg, scores, NEG_FILL)
    row_top = jnp.max(scores, axis=1, keepdims=True)
    expo = jnp.exp(scores - row_top)
    row_total = jnp.sum(expo, axis=1, keepdims=True)
    probs_low = (expo / row_total).astype(jnp.bfloat16)
    mixed = jnp.dot(probs_low, v_head, preferred_element_type=jnp.float32)
    return (mixed, row_top[:, 0] + jnp.log(row_total[:, 0]))


def head_backward(q_head, k_head, v_head, grad_mixed, log_total, same_seg):
    scores = contract(q_head, k_head, 1, 1) * HDIM ** (-0.5)
    scores = jnp.where(same_seg, scores, NEG_FILL)
    probs = jnp.exp(scores - log_total[:, None])
    probs_low = probs.astype(jnp.bfloat16)
    grad_values = contract(probs_low, grad_mixed, 0, 0)
    grad_probs = contract(grad_mixed, v_head, 1, 1)
    grad_scores = probs * (grad_probs - jnp.sum(probs * grad_probs, axis=1, keepdims=True))
    scores_low = grad_scores.astype(jnp.bfloat16)
    grad_query = jnp.dot(scores_low, k_head, preferred_element_type=jnp.float32) * HDIM ** (-0.5)
    grad_keys = contract(scores_low, q_head, 0, 0) * HDIM ** (-0.5)
    return (grad_query, grad_keys, grad_values)


def on_device(
    tokens,
    latents,
    grad_block,
    grad_head,
    image_lengths,
    ln1_gain,
    ln1_bias,
    w_qkv,
    b_qv,
    w_out,
    b_out,
    ln2_gain,
    ln2_bias,
    w_up,
    b_up,
    w_down,
    b_down,
    w_mod,
    b_mod,
    w_hid1,
    b_hid1,
    w_hid2,
    b_hid2,
):
    slot_len = LONG + BUF
    groups = image_lengths.shape[0]
    heads_here = w_qkv.shape[2] // HDIM
    model_width = tokens.shape[1]
    head_width = latents.shape[1]
    wq_full, wo_full, wu_full, wd_full, wm_full, wh1_full, wh2_full = (
        lax.all_gather(w_qkv, "dp", axis=1, tiled=True),
        lax.all_gather(w_out, "dp", axis=0, tiled=True),
        lax.all_gather(w_up, "dp", axis=0, tiled=True),
        lax.all_gather(w_down, "dp", axis=0, tiled=True),
        lax.all_gather(w_mod, "dp", axis=1, tiled=True),
        lax.all_gather(w_hid1, "dp", axis=0, tiled=True),
        lax.all_gather(w_hid2, "dp", axis=0, tiled=True),
    )
    segment, valid_row, image_row = jax.vmap(slot_masks)(image_lengths)
    valid_col = valid_row.reshape(-1, 1)
    image_col = image_row.reshape(-1, 1)

    def split_heads(flat):
        return jnp.transpose(flat.reshape(groups, slot_len, heads_here, HDIM), (0, 2, 1, 3))

    def join_heads(split):
        return jnp.transpose(split, (0, 2, 1, 3)).reshape(groups * slot_len, heads_here * HDIM)

    def slot_squares(values):
        squared = (values * values).reshape(groups, slot_len, -1)
        return jnp.sum(squared * valid_row[:, :, None], axis=(1, 2))

    tok_in = tokens.astype(jnp.float32)
    normed_one, inv_one = norm_parts(tok_in)
    norm_one = (normed_one * ln1_gain + ln1_bias).astype(jnp.bfloat16)
    proj_all = jnp.einsum("rd,tde->tre", norm_one, wq_full, preferred_element_type=jnp.float32)
    bias_rows = jnp.stack([b_qv[0], jnp.zeros_like(b_qv[0]), b_qv[1]])
    qkv_low = (proj_all + bias_rows[:, None, :]).astype(jnp.bfloat16)
    q_split = split_heads(qkv_low[0])
    k_split = split_heads(qkv_low[1])
    v_split = split_heads(qkv_low[2])

    def slot_forward(slot_in):
        q_slot, k_slot, v_slot, seg_slot = slot_in
        same_seg = seg_slot[:, None] == seg_slot[None, :]

        def one_head(head_in):
            return head_forward(head_in[0], head_in[1], head_in[2], same_seg)

        return lax.map(one_head, (q_slot, k_slot, v_slot))

    mixed_split, log_totals = lax.map(slot_forward, (q_split, k_split, v_split, segment))
    mixed_low = join_heads(mixed_split).astype(jnp.bfloat16)
    attn_out = (
        lax.psum(contract(mixed_low, wo_full, 1, 1).astype(jnp.bfloat16), "tp").astype(jnp.float32)
        + b_out
    )
    resid_one = tok_in + attn_out
    normed_two, inv_two = norm_parts(resid_one)
    norm_two = (normed_two * ln2_gain + ln2_bias).astype(jnp.bfloat16)
    pre_up = jnp.dot(norm_two, wu_full, preferred_element_type=jnp.float32) + b_up
    act_low = jax.nn.gelu(pre_up, approximate=False).astype(jnp.bfloat16)
    mlp_out = (
        lax.psum(contract(act_low, wd_full, 1, 1).astype(jnp.bfloat16), "tp").astype(jnp.float32)
        + b_down
    )
    block_rows = resid_one + mlp_out
    cond_low = jax.nn.silu(block_rows).astype(jnp.bfloat16)
    mod_all = (
        jnp.einsum("rd,tde->tre", cond_low, wm_full, preferred_element_type=jnp.float32)
        + b_mod[:, None, :]
    )
    lat_in = latents.astype(jnp.float32)
    lat_norm, lat_inv = norm_parts(lat_in)
    hid_in = (lat_norm * (1.0 + mod_all[1]) + mod_all[0]).astype(jnp.bfloat16)
    pre_hid = jnp.dot(hid_in, wh1_full, preferred_element_type=jnp.float32) + b_hid1
    hidden = jax.nn.silu(pre_hid).astype(jnp.bfloat16)
    branch = (
        lax.psum(contract(hidden, wh2_full, 1, 1).astype(jnp.bfloat16), "tp").astype(jnp.float32)
        + b_hid2
    )
    head_branch = mod_all[2] * branch
    head_out = lat_in + head_branch
    slot_stats = jnp.stack(
        [
            slot_squares(block_rows),
            slot_squares(attn_out),
            slot_squares(mlp_out),
            slot_squares(head_branch),
        ],
        axis=1,
    )
    slot_counts = jnp.sum(valid_row, axis=1)
    widths = jnp.array([model_width, model_width, model_width, head_width], jnp.float32)
    rms_values = jnp.sqrt(slot_stats / (slot_counts[:, None] * widths[None, :]))
    wq_full, wo_full, wu_full, wd_full, wm_full, wh1_full, wh2_full = (
        lax.all_gather(w_qkv, "dp", axis=1, tiled=True),
        lax.all_gather(w_out, "dp", axis=0, tiled=True),
        lax.all_gather(w_up, "dp", axis=0, tiled=True),
        lax.all_gather(w_down, "dp", axis=0, tiled=True),
        lax.all_gather(w_mod, "dp", axis=1, tiled=True),
        lax.all_gather(w_hid1, "dp", axis=0, tiled=True),
        lax.all_gather(w_hid2, "dp", axis=0, tiled=True),
    )
    grad_rows = grad_block.astype(jnp.float32) * valid_col
    grad_head_rows = grad_head.astype(jnp.float32) * image_col
    grad_branch = grad_head_rows * mod_all[2]
    d_b_hid2 = jnp.sum(grad_branch, axis=0)
    branch_low = grad_branch.astype(jnp.bfloat16)
    d_w_hid2 = contract(branch_low, hidden, 0, 0)
    grad_hidden = jnp.dot(branch_low, wh2_full, preferred_element_type=jnp.float32)
    grad_pre_hid = jax.vjp(jax.nn.silu, pre_hid)[1](grad_hidden)[0]
    d_b_hid1 = jnp.sum(grad_pre_hid, axis=0)
    pre_hid_low = grad_pre_hid.astype(jnp.bfloat16)
    d_w_hid1 = contract(hid_in, pre_hid_low, 0, 0)
    grad_hid_in = lax.psum(contract(pre_hid_low, wh1_full, 1, 1).astype(jnp.bfloat16), "tp").astype(
        jnp.float32
    )
    grad_mod = jnp.stack([grad_hid_in, grad_hid_in * lat_norm, grad_head_rows * branch])
    d_b_mod = jnp.sum(grad_mod, axis=1)
    mod_low = grad_mod.astype(jnp.bfloat16)
    d_w_mod = jnp.einsum("rd,tre->tde", cond_low, mod_low, preferred_element_type=jnp.float32)
    grad_cond = jnp.einsum("tre,tde->rd", mod_low, wm_full, preferred_element_type=jnp.float32)
    grad_latents = grad_head_rows + norm_back(grad_hid_in * (1.0 + mod_all[1]), lat_norm, lat_inv)
    grad_block_all = grad_rows + jax.vjp(jax.nn.silu, block_rows)[1](grad_cond)[0]
    d_b_down = jnp.sum(grad_block_all, axis=0)
    block_low = grad_block_all.astype(jnp.bfloat16)
    d_w_down = contract(block_low, act_low, 0, 0)
    grad_act = jnp.dot(block_low, wd_full, preferred_element_type=jnp.float32)
    grad_pre_up = jax.vjp(lambda inner: jax.nn.gelu(inner, approximate=False), pre_up)[1](grad_act)[
        0
    ]
    d_b_up = jnp.sum(grad_pre_up, axis=0)
    up_low = grad_pre_up.astype(jnp.bfloat16)
    d_w_up = contract(norm_two, up_low, 0, 0)
    grad_norm_two = lax.psum(contract(up_low, wu_full, 1, 1).astype(jnp.bfloat16), "tp").astype(
        jnp.float32
    )
    d_ln2_gain = jnp.sum(grad_norm_two * normed_two, axis=0)
    d_ln2_bias = jnp.sum(grad_norm_two, axis=0)
    grad_resid = grad_block_all + norm_back(grad_norm_two * ln2_gain, normed_two, inv_two)
    d_b_out = jnp.sum(grad_resid, axis=0)
    resid_low = grad_resid.astype(jnp.bfloat16)
    d_w_out = contract(resid_low, mixed_low, 0, 0)
    grad_mixed = jnp.dot(resid_low, wo_full, preferred_element_type=jnp.float32).astype(
        jnp.bfloat16
    )

    def slot_backward(slot_in):
        q_slot, k_slot, v_slot, g_slot, lse_slot, seg_slot = slot_in
        same_seg = seg_slot[:, None] == seg_slot[None, :]

        def one_head(head_in):
            return head_backward(
                head_in[0], head_in[1], head_in[2], head_in[3], head_in[4], same_seg
            )

        return lax.map(one_head, (q_slot, k_slot, v_slot, g_slot, lse_slot))

    grad_q, grad_k, grad_v = lax.map(
        slot_backward, (q_split, k_split, v_split, split_heads(grad_mixed), log_totals, segment)
    )
    grad_q = join_heads(grad_q)
    grad_k = join_heads(grad_k)
    grad_v = join_heads(grad_v)
    d_b_qv = jnp.stack([jnp.sum(grad_q, axis=0), jnp.sum(grad_v, axis=0)])
    proj_low = jnp.stack([grad_q, grad_k, grad_v]).astype(jnp.bfloat16)
    d_w_qkv = jnp.einsum("rd,tre->tde", norm_one, proj_low, preferred_element_type=jnp.float32)
    grad_norm_one = lax.psum(
        jnp.einsum("tre,tde->rd", proj_low, wq_full, preferred_element_type=jnp.float32).astype(
            jnp.bfloat16
        ),
        "tp",
    ).astype(jnp.float32)
    d_ln1_gain = jnp.sum(grad_norm_one * normed_one, axis=0)
    d_ln1_bias = jnp.sum(grad_norm_one, axis=0)
    grad_tokens = grad_resid + norm_back(grad_norm_one * ln1_gain, normed_one, inv_one)
    d_w_qkv, d_w_out, d_w_up, d_w_down, d_w_mod, d_w_hid1, d_w_hid2 = (
        lax.psum_scatter(d_w_qkv, "dp", scatter_dimension=1, tiled=True),
        lax.psum_scatter(d_w_out, "dp", scatter_dimension=0, tiled=True),
        lax.psum_scatter(d_w_up, "dp", scatter_dimension=0, tiled=True),
        lax.psum_scatter(d_w_down, "dp", scatter_dimension=0, tiled=True),
        lax.psum_scatter(d_w_mod, "dp", scatter_dimension=1, tiled=True),
        lax.psum_scatter(d_w_hid1, "dp", scatter_dimension=0, tiled=True),
        lax.psum_scatter(d_w_hid2, "dp", scatter_dimension=0, tiled=True),
    )
    (
        d_ln1_gain,
        d_ln1_bias,
        d_b_qv,
        d_b_out,
        d_ln2_gain,
        d_ln2_bias,
        d_b_up,
        d_b_down,
        d_b_mod,
        d_b_hid1,
        d_b_hid2,
    ) = lax.psum(
        (
            d_ln1_gain,
            d_ln1_bias,
            d_b_qv,
            d_b_out,
            d_ln2_gain,
            d_ln2_bias,
            d_b_up,
            d_b_down,
            d_b_mod,
            d_b_hid1,
            d_b_hid2,
        ),
        "dp",
    )
    return (
        block_rows.astype(jnp.bfloat16),
        head_out.astype(jnp.bfloat16),
        grad_tokens,
        grad_latents,
        d_ln1_gain,
        d_ln1_bias,
        d_w_qkv,
        d_b_qv,
        d_w_out,
        d_b_out,
        d_ln2_gain,
        d_ln2_bias,
        d_w_up,
        d_b_up,
        d_w_down,
        d_b_down,
        d_w_mod,
        d_b_mod,
        d_w_hid1,
        d_b_hid1,
        d_w_hid2,
        d_b_hid2,
        rms_values,
    )


def solution(mesh):
    placed = (
        P("dp", None),
        P("dp", None),
        P("dp", None),
        P("dp", None),
        P("dp", None),
        P(),
        P(),
        P(None, "dp", "tp"),
        P(None, "tp"),
        P("dp", "tp"),
        P(),
        P(),
        P(),
        P("dp", "tp"),
        P("tp"),
        P("dp", "tp"),
        P(),
        P(None, "dp", None),
        P(),
        P("dp", "tp"),
        P("tp"),
        P("dp", "tp"),
        P(),
    )
    return jax.shard_map(
        on_device,
        mesh=mesh,
        in_specs=placed,
        out_specs=(
            P("dp", None),
            P("dp", None),
            P("dp", None),
            P("dp", None),
            P(),
            P(),
            P(None, "dp", "tp"),
            P(None, "tp"),
            P("dp", "tp"),
            P(),
            P(),
            P(),
            P("dp", "tp"),
            P("tp"),
            P("dp", "tp"),
            P(),
            P(None, "dp", None),
            P(),
            P("dp", "tp"),
            P("tp"),
            P("dp", "tp"),
            P(),
            P("dp", None),
        ),
        check_vma=False,
    )
```

profile of v0, /device:TPU:0, one launch (start us, length us, event | category | flops | bytes accessed | tf_op | source)
XLA Modules:
  0.0 1509.5 jit_solution(3345618830632234657)
XLA Ops:
  12.0 26.5 %all_gather.29 = bf16[768,384]{1,0:T(8,128)(2,1)} all-gather(bf16[48,384]{1,0:T(8,128)(2,1)S(1)} %copy-done.26), channel_id=1, replica_groups=mesh['dp'=16,'tp'=2] {'dp'}, dimensions={0}, use_global_device_ids=true | all-gather | bytes 626688 | tf_op jit(solution)/shard_map/all_gather | solution.py:105
  38.6 15.7 %all-gather.7.cloned.1.call-done = bf16[3,768,384]{2,1,0:T(8,128)(2,1)} async-done(((bf16[3,48,384]{2,1,0:T(8,128)(2,1)}), bf16[3,768,384]{2,1,0:T(8,128)(2,1)}) %all-gather.7.cloned.1.call-update) | async-done | bytes 1769488 | tf_op jit(solution)/shard_map/all_gather | solution.py:104
  71.7 39.7 %while.50 = (s32[]{:T(128)}, bf16[6,1088,64]{1,2,0:T(8,128)(2,1)}, f32[6,1088]{1,0:T(8,128)}, bf16[6,1088,64]{2,1,0:T(8,128)(2,1)}, bf16[6,1088,64]{2,1,0:T(8,12...) while((s32[]{:T(128)}, bf16[6,1088,64]{1,2,0:T(8,128)(2,1)}, ...), condition=%wide.region_7.8_spmd.clone.clone, body=%wide.region_4.7_spmd.clone.sunk.clone | while | flops 313691072 | bytes 15406169 | solution.py:143
  118.5 49.9 %all-reduce.12.cloned.1.call-done = bf16[1088,768]{1,0:T(8,128)(2,1)} async-done(((bf16[1088,768]{1,0:T(8,128)(2,1)}), bf16[1088,768]{1,0:T(8,128)(2,1)}) %all-reduce.12.cloned.1.call-update) | async-done | bytes 1671184 | tf_op jit(solution)/shard_map/psum | solution.py:148
  172.8 40.1 %all-gather.9.cloned.1.call-done = bf16[768,1536]{1,0:T(8,128)(2,1)} async-done(((bf16[48,1536]{1,0:T(8,128)(2,1)}), bf16[768,1536]{1,0:T(8,128)(2,1)}) %all-gather.9.cloned.1.call-update) | async-done | bytes 2359312 | tf_op jit(solution)/shard_map/all_gather | solution.py:106
  212.9 20.9 %multiply_convert_fusion.1 = (bf16[1088,1536]{1,0:T(8,128)(2,1)}, f32[1088,1536]{1,0:T(8,128)}, f32[1088,1536]{1,0:T(8,128)}) fusion(f32[1536]{0:T(1024)S(1)} %copy-done.40, bf16[768,1536]{1,0:T(8,128)(2,1)} %all-gather.9.cloned.1.call-done, f32[768]{0:T(1024)S(1)} %copy-done.43, f32[768]{0:T(1024)S(1)} %copy-done.27, f32[1088]{0:T(1024)S(1)} %add_rsqrt_fusion.1, ...), kind=kOutput, calls=%fused_computation.70 | convolution fusion | flops 2684731392 | bytes 22437376 | tf_op jit(solution)/shard_map/dot_general | solution.py:154
  233.8 22.3 %all-gather.11.cloned.1.call-done = bf16[768,1536]{1,0:T(8,128)(2,1)} async-done(((bf16[48,1536]{1,0:T(8,128)(2,1)}), bf16[768,1536]{1,0:T(8,128)(2,1)}) %all-gather.11.cloned.1.call-update) | async-done | bytes 2359312 | tf_op jit(solution)/shard_map/all_gather | solution.py:107
  256.1 6.7 convolution_convert_fusion.4
  269.4 46.0 %all-reduce.14.cloned.1.call-done = bf16[1088,768]{1,0:T(8,128)(2,1)} async-done(((bf16[1088,768]{1,0:T(8,128)(2,1)}), bf16[1088,768]{1,0:T(8,128)(2,1)}) %all-reduce.14.cloned.1.call-update) | async-done | bytes 1671184 | tf_op jit(solution)/shard_map/psum | solution.py:157
  315.4 55.6 %all-gather.13.cloned.1.call-done = bf16[3,768,1024]{2,1,0:T(8,128)(2,1)} async-done(((bf16[3,48,1024]{2,1,0:T(8,128)(2,1)}), bf16[3,768,1024]{2,1,0:T(8,128)(2,1)}) %all-gather.13.cloned.1.call-update) | async-done | bytes 4718608 | tf_op jit(solution)/shard_map/all_gather | solution.py:108
  371.0 9.3 add_bitcast_fusion
  388.1 21.5 %all-gather.17.cloned.1.call-done = bf16[1024,512]{1,0:T(8,128)(2,1)} async-done(((bf16[64,512]{1,0:T(8,128)(2,1)}), bf16[1024,512]{1,0:T(8,128)(2,1)}) %all-gather.17.cloned.1.call-update) | async-done | bytes 1048592 | tf_op jit(solution)/shard_map/all_gather | solution.py:110
  414.3 34.5 %all-gather.15.cloned.1.call-done = bf16[1024,512]{1,0:T(8,128)(2,1)} async-done(((bf16[64,512]{1,0:T(8,128)(2,1)}), bf16[1024,512]{1,0:T(8,128)(2,1)}) %all-gather.15.cloned.1.call-update) | async-done | bytes 1048592 | tf_op jit(solution)/shard_map/all_gather | solution.py:109
  460.0 112.5 %all-reduce.22.cloned.1.call-done = (bf16[1088,1024]{1,0:T(8,128)(2,1)}, bf16[1088,1024]{1,0:T(8,128)(2,1)}) async-done(((bf16[1088,1024]{1,0:T(8,128)(2,1)}, bf16[1088,1024]{1,0:T(8,128)(2,1)}), (bf16[1088,1024]{1,0:T(8,128)(2,1)}, bf16[1088,1024]{1,0:T(8,128)(2,1)})) %all-reduce.22.cloned.1.call-update) | async-done | bytes 4456464 | tf_op jit(solution)/shard_map/psum | solution.py:172
  577.1 9.2 multiply_reduce_fusion.1
  586.3 8.0 fusion.76
  594.3 11.2 fusion.102
  605.5 9.6 fusion.152
  621.0 53.5 %all-reduce.16.cloned.1.call-done = bf16[1088,768]{1,0:T(8,128)(2,1)} async-done(((bf16[1088,768]{1,0:T(8,128)(2,1)}), bf16[1088,768]{1,0:T(8,128)(2,1)}) %all-reduce.16.cloned.1.call-update) | async-done | bytes 1671184 | tf_op jit(solution)/shard_map/psum | solution.py:229
  674.5 7.1 fusion.103
  689.7 79.5 %while.51 = (s32[]{:T(128)}, f32[6,1088,64]{1,2,0:T(8,128)}, bf16[6,1088,64]{1,2,0:T(8,128)(2,1)}, f32[6,1088,64]{1,2,0:T(8,128)}, bf16[6,1088,64]{2,1,0:T(8,128...) while((s32[]{:T(128)}, f32[6,1088,64]{1,2,0:T(8,128)}, ...), condition=%wide.region_22.23_spmd.clone.clone, body=%wide.region_20.22_spmd.clone.sunk.clone | while | flops 769571776 | bytes 38410352 | solution.py:251
  787.0 13.7 convolution_bitcast_fusion.2
  800.7 14.0 copy.105
  842.4 7.2 fusion.113
  849.7 9.4 fusion.120
  876.5 65.8 %all-reduce.2 = (f32[768]{0:T(1024)}, f32[768]{0:T(1024)}, f32[2,384]{1,0:T(2,128)}, f32[768]{0:T(1024)}, f32[768]{0:T(1024)}, /*index=5*/f32[768]{0:T(1024)}, f...) all-reduce(f32[768]{0:T(1024)S(1)} %get-tuple-element.362, ...), channel_id=1, replica_groups=mesh['dp'=16,'tp'=2] {'dp'}, use_global_device_ids=true, to_apply=%region_29.30 | all-reduce | flops 11520 | bytes 92160 | tf_op jit(solution)/shard_map/psum | solution.py:292
  946.2 205.2 %all-reduce.20.cloned.1.call-done = (f32[3,768,384]{2,0,1:T(4,128)}, f32[3,768,1024]{2,0,1:T(4,128)}) async-done(((f32[3,768,384]{2,0,1:T(4,128)}, f32[3,768,1024]{2,0,1:T(4,128)}), (f32[3,768,384]{2,0,1:T(4,128)}, f32[3,768,1024]{2,0,1:T(4,128)})) %all-reduce.20.cloned.1.call-update) | async-done | bytes 12976144
  1155.6 62.3 %reduce-scatter.12.cloned.1.call-done = f32[64,512]{1,0:T(8,128)} async-done(((f32[1024,512]{1,0:T(8,128)}), f32[64,512]{1,0:T(8,128)}) %reduce-scatter.12.cloned.1.call-update) | async-done | bytes 131088 | tf_op jit(solution)/shard_map/reduce_scatter | solution.py:277
  1217.8 64.7 %reduce-scatter.14.cloned.1.call-done = f32[64,512]{1,0:T(8,128)} async-done(((f32[1024,512]{1,0:T(8,128)}), f32[64,512]{1,0:T(8,128)}) %reduce-scatter.14.cloned.1.call-update) | async-done | bytes 131088 | tf_op jit(solution)/shard_map/reduce_scatter | solution.py:278
  1282.6 61.6 %reduce-scatter.6.cloned.1.call-done = f32[48,384]{1,0:T(8,128)} async-done(((f32[768,384]{1,0:T(8,128)}), f32[48,384]{1,0:T(8,128)}) %reduce-scatter.6.cloned.1.call-update) | async-done | bytes 73744 | tf_op jit(solution)/shard_map/reduce_scatter | solution.py:273
  1344.1 79.4 %reduce-scatter.8.cloned.1.call-done = f32[48,1536]{1,0:T(8,128)} async-done(((f32[768,1536]{1,0:T(8,128)}), f32[48,1536]{1,0:T(8,128)}) %reduce-scatter.8.cloned.1.call-update) | async-done | bytes 294928 | tf_op jit(solution)/shard_map/reduce_scatter | solution.py:274
  1423.6 78.9 %reduce-scatter.10.cloned.1.call-done = f32[48,1536]{1,0:T(8,128)} async-done(((f32[768,1536]{1,0:T(8,128)}), f32[48,1536]{1,0:T(8,128)}) %reduce-scatter.10.cloned.1.call-update) | async-done | bytes 294928 | tf_op jit(solution)/shard_map/reduce_scatter | solution.py:275
  (290 shorter events, 271.4 us)
Async XLA Ops:
  7.2 47.1 %all-gather.7.cloned.1.call-start = ((), (), s32[]{:S(2)}) async-start(), calls=%async_computation.5 | async-start | bytes 1880064 | tf_op jit(solution)/shard_map/all_gather | solution.py:104
  8.0 160.4 %all-reduce.12.cloned.1.call-start = ((), (), s32[]{:S(2)}) async-start(), calls=%async_computation.6 | async-start | bytes 3342336 | tf_op jit(solution)/shard_map/psum | solution.py:148
  8.0 46.3 %copy-start.28 = (f32[768]{0:T(1024)S(1)}, f32[768]{0:T(1024)}, u32[]{:S(2)}) copy-start(f32[768]{0:T(1024)} %param.33) | copy-start | bytes 9220
  8.0 46.3 %copy-start.41 = (f32[768]{0:T(1024)S(1)}, f32[768]{0:T(1024)}, u32[]{:S(2)}) copy-start(f32[768]{0:T(1024)} %param.34) | copy-start | bytes 9220
  11.4 47.1 %copy-start.21 = (f32[1088]{0:T(1024)}, f32[1088]{0:T(1024)S(1)}, u32[]{:S(2)}) copy-start(f32[1088]{0:T(1024)S(1)} %broadcast_multiply_fusion.8) | copy-start | bytes 13060
  12.0 46.4 %copy-start.23 = (f32[1088]{0:T(1024)}, f32[1088]{0:T(1024)S(1)}, u32[]{:S(2)}) copy-start(f32[1088]{0:T(1024)S(1)} %add_rsqrt_fusion.2) | copy-start | bytes 13060
  111.4 56.9 %copy-start.25 = (f32[768]{0:T(1024)S(1)}, f32[768]{0:T(1024)}, u32[]{:S(2)}) copy-start(f32[768]{0:T(1024)} %param.38) | copy-start | bytes 9220
  115.6 97.2 %all-gather.9.cloned.1.call-start = ((), (), s32[]{:S(2)}) async-start(), calls=%async_computation.7 | async-start | bytes 2506752 | tf_op jit(solution)/shard_map/all_gather | solution.py:106
  116.4 139.8 %all-gather.11.cloned.1.call-start = ((), (), s32[]{:S(2)}) async-start(), calls=%async_computation.8 | async-start | bytes 2506752 | tf_op jit(solution)/shard_map/all_gather | solution.py:107
  116.9 198.5 %all-reduce.14.cloned.1.call-start = ((), (), s32[]{:S(2)}) async-start(), calls=%async_computation.9 | async-start | bytes 3342336 | tf_op jit(solution)/shard_map/psum | solution.py:157
  118.4 94.4 %copy-start.27 = (f32[768]{0:T(1024)S(1)}, f32[768]{0:T(1024)}, u32[]{:S(2)}) copy-start(f32[768]{0:T(1024)} %param.39) | copy-start | bytes 9220
  118.4 94.4 %copy-start.40 = (f32[1536]{0:T(1024)S(1)}, f32[1536]{0:T(1024)}, u32[]{:S(2)}) copy-start(f32[1536]{0:T(1024)} %param.42) | copy-start | bytes 18436
  118.4 94.4 %copy-start.43 = (f32[768]{0:T(1024)S(1)}, f32[768]{0:T(1024)}, u32[]{:S(2)}) copy-start(f32[768]{0:T(1024)} %param.40) | copy-start | bytes 9220
  262.8 108.2 %copy-start.31 = (f32[768]{0:T(1024)S(1)}, f32[768]{0:T(1024)}, u32[]{:S(2)}) copy-start(f32[768]{0:T(1024)} %param.44) | copy-start | bytes 9220
  262.8 108.2 %copy-start.39 = (f32[3,1024]{1,0:T(4,128)S(1)}, f32[3,1024]{1,0:T(4,128)}, u32[]{:S(2)}) copy-start(f32[3,1024]{1,0:T(4,128)} %param.46) | copy-start | bytes 36868
  262.8 108.2 %all-gather.13.cloned.1.call-start = ((), (), s32[]{:S(2)}) async-start(), calls=%async_computation.10 | async-start | bytes 5013504 | tf_op jit(solution)/shard_map/all_gather | solution.py:108
  263.4 146.3 %all-gather.17.cloned.1.call-start = ((), (), s32[]{:S(2)}) async-start(), calls=%async_computation.12 | async-start | bytes 1114112 | tf_op jit(solution)/shard_map/all_gather | solution.py:110
  264.1 184.6 %all-gather.15.cloned.1.call-start = ((), (), s32[]{:S(2)}) async-start(), calls=%async_computation.11 | async-start | bytes 1114112 | tf_op jit(solution)/shard_map/all_gather | solution.py:109
  264.9 307.6 %all-reduce.22.cloned.1.call-start = ((), (), s32[]{:S(2)}) async-start(), calls=%async_computation.21 | async-start | bytes 8912896 | tf_op jit(solution)/shard_map/psum | solution.py:172
  371.0 14.1 copy-start.7
  409.7 39.1 %copy-start.45 = (f32[512]{0:T(512)S(1)}, f32[512]{0:T(512)}, u32[]{:S(2)}) copy-start(f32[512]{0:T(512)} %param.48) | copy-start | bytes 6148
  459.6 115.2 %copy-start.32 = (f32[1024]{0:T(1024)S(1)}, f32[1024]{0:T(1024)}, u32[]{:S(2)}) copy-start(f32[1024]{0:T(1024)} %param.50) | copy-start | bytes 12292
  459.6 215.0 %all-reduce.16.cloned.1.call-start = ((), (), s32[]{:S(2)}) async-start(), calls=%async_computation.13 | async-start | bytes 3342336 | tf_op jit(solution)/shard_map/psum | solution.py:229
  574.8 19.5 %copy-start.10 = (f32[1,1088,1024]{2,1,0:T(8,128)}, f32[1,1088,1024]{2,1,0:T(8,128)S(1)}, u32[]{:S(2)}) copy-start(f32[1,1088,1024]{2,1,0:T(8,128)S(1)} %convert_bitcast_fusion) | copy-start | bytes 13369348
  620.8 252.4 %all-reduce.18.cloned.1.call-start = ((), (), s32[]{:S(2)}) async-start(), calls=%async_computation.14 | async-start | bytes 3342336 | tf_op jit(solution)/shard_map/psum | solution.py:262
  786.7 364.7 %all-reduce.20.cloned.1.call-start = ((), (), s32[]{:S(2)}) async-start(), calls=%async_computation.20 | async-start | bytes 34603008
  827.4 390.4 %reduce-scatter.12.cloned.1.call-start = ((), (), s32[]{:S(2)}) async-start(), calls=%async_computation.18 | async-start | bytes 2228224 | tf_op jit(solution)/shard_map/reduce_scatter | solution.py:277
  832.3 450.2 %reduce-scatter.14.cloned.1.call-start = ((), (), s32[]{:S(2)}) async-start(), calls=%async_computation.19 | async-start | bytes 2228224 | tf_op jit(solution)/shard_map/reduce_scatter | solution.py:278
  837.7 506.4 %reduce-scatter.6.cloned.1.call-start = ((), (), s32[]{:S(2)}) async-start(), calls=%async_computation.15 | async-start | bytes 1253376 | tf_op jit(solution)/shard_map/reduce_scatter | solution.py:273
  842.1 581.4 %reduce-scatter.8.cloned.1.call-start = ((), (), s32[]{:S(2)}) async-start(), calls=%async_computation.16 | async-start | bytes 5013504 | tf_op jit(solution)/shard_map/reduce_scatter | solution.py:274
  849.6 652.9 %reduce-scatter.10.cloned.1.call-start = ((), (), s32[]{:S(2)}) async-start(), calls=%async_computation.17 | async-start | bytes 5013504 | tf_op jit(solution)/shard_map/reduce_scatter | solution.py:275
  873.1 69.2 %copy-start.18 = (bf16[1088,768]{1,0:T(8,128)(2,1)S(1)}, bf16[1088,768]{1,0:T(8,128)(2,1)}, u32[]{:S(2)}) copy-start(bf16[1088,768]{1,0:T(8,128)(2,1)} %all-reduce.18.cloned.1.call-done) | copy-start | bytes 5013508
  (35 other events, 210.2 us)
Sparse Core Ops, SparseCore 0:
  10.4 43.8 all-gather.6
  115.8 52.5 all-reduce.11
  170.6 42.2 all-gather.8
  215.0 41.0 all-gather.10
  262.9 52.4 all-reduce.13
  317.5 53.4 all-gather.12
  373.2 36.4 all-gather.16
  411.8 36.8 all-gather.14
  459.7 112.7 all-reduce.21
  620.9 53.6 all-reduce.15
  786.9 53.6 all-reduce.17
  845.1 306.2 all-reduce.19
  1156.2 61.6 reduce-scatter.11
  1222.0 60.5 reduce-scatter.13
  1287.0 57.0 reduce-scatter.5
  1348.9 74.6 reduce-scatter.7
  1427.8 74.5 reduce-scatter.9
where the time goes:
time: 1520 us; the launch traced here: 1510 us
  waiting for transfers between devices  1010 us (66%)
  matrix products  242 us (16%)
  blocking collectives  92.3 us (6%)
  other arithmetic  74.9 us (5%)
  local copies, waits for them, and re-layouts  74.6 us (5%)
  between operations  15.6 us (1%)
    unnamed x18, waiting for transfers between devices  209 us
    dot_general x40, matrix products, contract(): lax.dot_general(left, right, (((left_dim,), (right_dim,)), ((), ())), pre...  120 us
    psum x1, waiting for transfers between devices, on_device(): lax.psum(contract(hidden, wh2_full, 1, 1).astype(jnp.bfloat16), 'tp')  112 us
    reduce_scatter x1, waiting for transfers between devices, on_device(): lax.psum_scatter(d_w_up, 'dp', scatter_dimension=0, tiled=True)  79.4 us
    reduce_scatter x1, waiting for transfers between devices, on_device(): lax.psum_scatter(d_w_down, 'dp', scatter_dimension=0, tiled=True)  78.9 us
    psum x1, blocking collectives, on_device(): lax.psum((d_ln1_gain, d_ln1_bias, d_b_qv, d_b_out, d_ln2_gain, d_ln2_bias...  65.8 us
    reduce_scatter x1, waiting for transfers between devices, on_device(): lax.psum_scatter(d_w_hid2, 'dp', scatter_dimension=0, tiled=True)  64.7 us
    reduce_scatter x1, waiting for transfers between devices, on_device(): lax.psum_scatter(d_w_hid1, 'dp', scatter_dimension=0, tiled=True)  62.3 us
  transfers between devices with their start and end apart: 17, of which 16 were waited for; matrix products, arithmetic and copies ran while one was open for 10% of the time, Pallas kernels for 0%

commit v1 on v0

v1 whole, which is shorter than its diff:
```python
import functools

import jax
import jax.numpy as jnp
from jax import lax
from jax.experimental import pallas as pl
from jax.experimental.pallas import tpu as pltpu
from jax.sharding import PartitionSpec as P

HDIM = 64
BUF = 64
LONG = 1024
EPS_NORM = 1e-06
FAR = -1e30
VMEM_LIMIT = 60 * 1024 * 1024
F32 = jnp.float32
LOW = jnp.bfloat16


def params():
    return pltpu.CompilerParams(vmem_limit_bytes=VMEM_LIMIT)


def dot_nn(a, b):
    return lax.dot_general(a, b, (((1,), (0,)), ((), ())), preferred_element_type=F32)


def dot_nt(a, b):
    return lax.dot_general(a, b, (((1,), (1,)), ((), ())), preferred_element_type=F32)


def dot_tn(a, b):
    return lax.dot_general(a, b, (((0,), (0,)), ((), ())), preferred_element_type=F32)


def norm_parts(values):
    row_mean = jnp.mean(values, axis=-1, keepdims=True)
    centred = values - row_mean
    inv_dev = lax.rsqrt(jnp.mean(centred * centred, axis=-1, keepdims=True) + EPS_NORM)
    return centred * inv_dev, inv_dev


def norm_back(grad_norm, normed, inv_dev):
    mean_grad = jnp.mean(grad_norm, axis=-1, keepdims=True)
    mean_cross = jnp.mean(grad_norm * normed, axis=-1, keepdims=True)
    return inv_dev * (grad_norm - mean_grad - normed * mean_cross)


def gelu_parts(x):
    z = jnp.abs(x) * 0.7071067811865476
    t = 1.0 / (1.0 + 0.3275911 * z)
    e = jnp.exp(-z * z)
    poly = t * (
        0.254829592 + t * (-0.284496736 + t * (1.421413741 + t * (-1.453152027 + t * 1.061405429)))
    )
    tail = 0.5 * poly * e
    cdf = jnp.where(x >= 0, 1.0 - tail, tail)
    return x * cdf, cdf + x * (0.3989422804014327 * e)


def sigmoid(x):
    return 0.5 * jnp.tanh(0.5 * x) + 0.5


def flat(block):
    return block.reshape(block.shape[0] * block.shape[1], block.shape[2])


def colsum(values):
    return jnp.sum(values, axis=0, keepdims=True)


def qkv_kernel(tp, tok, gain, bias, w_own, w_oth, b_own, b_oth, norm_out, proj_out):
    normed, _ = norm_parts(tok[...].astype(F32))
    norm_one = (normed * gain[...] + bias[...]).astype(LOW)
    norm_out[...] = norm_one
    half = w_own.shape[-1]
    for side, (w, b) in enumerate(((w_own, b_own), (w_oth, b_oth))):
        for t in range(3):
            proj = dot_nn(norm_one, flat(w[:, 0, t]))
            if t == 0:
                low = ((proj + b[0:1]).astype(LOW).astype(F32) * HDIM ** (-0.5)).astype(LOW)
            elif t == 1:
                low = proj.astype(LOW)
            else:
                low = (proj + b[1:2]).astype(LOW)
            proj_out[t, :, side * half : (side + 1) * half] = low


def row_spec(rows, *tail):
    zeros = (0,) * len(tail)
    return pl.BlockSpec((rows, *tail), lambda i, tp: (i, *zeros))


def const_spec(*shape):
    zeros = (0,) * len(shape)
    return pl.BlockSpec(shape, lambda i, tp: zeros, pipeline_mode=pl.Buffered(1))


def side_spec(arr, count, first, other):
    dp, _, _, rows, cols = arr.shape
    block = (dp, 1, count, rows, cols)
    if other:
        return pl.BlockSpec(
            block, lambda i, tp: (0, 1 - tp[0], first // count, 0, 0), pipeline_mode=pl.Buffered(1)
        )
    return pl.BlockSpec(
        block, lambda i, tp: (0, tp[0], first // count, 0, 0), pipeline_mode=pl.Buffered(1)
    )


def sds(shape, dtype):
    return jax.ShapeDtypeStruct(shape, dtype)


def run(kernel, tp, steps, ins, outs, scratch=(), flops=0, nbytes=0, exps=0):
    return pl.pallas_call(
        kernel,
        grid_spec=pltpu.PrefetchScalarGridSpec(
            num_scalar_prefetch=1,
            grid=(steps,),
            in_specs=[spec for _, spec in ins],
            out_specs=[spec for _, spec in outs],
            scratch_shapes=list(scratch),
        ),
        out_shape=[shape for shape, _ in outs],
        compiler_params=params(),
        cost_estimate=pl.CostEstimate(flops=flops, bytes_accessed=nbytes, transcendentals=exps),
    )(tp, *[arr for arr, _ in ins])


def lanes():
    return lax.broadcasted_iota(jnp.int32, (1, 128), 1)


def attn_fwd_kernel(tp, q, k, v, seg_q, seg_k, mixed, total):
    rows = q.shape[0]
    chunk = rows // 4
    left = lanes() < HDIM
    k_all, v_all = k[...], v[...]
    one = jnp.ones_like(v_all)
    k_aug = (jnp.where(left, k_all, seg_k[...]), jnp.where(left, seg_k[...], k_all))
    v_aug = (jnp.where(left, v_all, one), jnp.where(left, one, v_all))

    def step(i, carry):
        at = pl.ds(pl.multiple_of(i * chunk, 16), chunk)
        q_part, seg_part = q[at, :], seg_q[at, :]
        q_aug = (jnp.where(left, q_part, seg_part), jnp.where(left, seg_part, q_part))
        outs = []
        for h in range(2):
            s = dot_nt(q_aug[h], k_aug[h])
            top = jnp.max(s, axis=1, keepdims=True)
            p = jnp.exp(s - top).astype(LOW)
            outs.append((dot_nn(p, v_aug[h]), top))
        mix = jnp.where(left, outs[0][0], outs[1][0])
        tot = jnp.where(left, outs[1][0], outs[0][0])
        tot = pltpu.roll(tot, HDIM, 1)
        mixed[at, :] = (mix / tot).astype(LOW)
        total[at, :] = jnp.where(left, outs[0][1], outs[1][1]) + jnp.log(tot)
        return carry

    lax.fori_loop(0, 4, step, 0)


def three_terms(value, at, base):
    lane = lanes() & (HDIM - 1)
    hi = value.astype(LOW)
    rest = value - hi.astype(F32)
    mid = rest.astype(LOW)
    low = (rest - mid.astype(F32)).astype(LOW)
    out = jnp.where(lane == at, hi, base)
    out = jnp.where(lane == at + 1, mid, out)
    return jnp.where(lane == at + 2, low, out)


def attn_bwd_kernel(
    tp, q, k, v, g, mixed, total, seg_q, seg_k, dproj, sums, q0, q1, g0, g1, dq_t
):
    rows = q.shape[0]
    chunk = rows // 4
    left = lanes() < HDIM
    lane = lanes() & (HDIM - 1)
    q_all, g_all = q[...], g[...]
    cross = g_all.astype(F32) * mixed[...].astype(F32)
    d_left = jnp.sum(jnp.where(left, cross, 0.0), axis=1, keepdims=True)
    d_right = jnp.sum(jnp.where(left, 0.0, cross), axis=1, keepdims=True)
    neg_total = -pltpu.roll(total[...], HDIM, 1)
    q_tail = three_terms(neg_total, 4, seg_q[...])
    g_tail = three_terms(
        jnp.where(left, -d_right, -d_left), 0, jnp.zeros_like(g_all)
    )
    q0[...] = jnp.where(left, q_all, q_tail)
    q1[...] = jnp.where(left, q_tail, q_all)
    g0[...] = jnp.where(left, g_all, g_tail)
    g1[...] = jnp.where(left, g_tail, g_all)
    dq_t[...] = jnp.zeros_like(dq_t)
    k_ones = jnp.where((lane >= 4) & (lane < 7), 1.0, 0.0).astype(LOW)
    v_ones = jnp.where(lane < 3, 1.0, 0.0).astype(LOW)
    sums[...] = jnp.zeros_like(sums)

    def step(i, carry):
        at = pl.ds(pl.multiple_of(i * chunk, 16), chunk)
        k_part, v_part = k[at, :], v[at, :]
        k_tail = seg_k[at, :] + k_ones
        v_tail = jnp.broadcast_to(v_ones, v_part.shape)
        zero = jnp.zeros_like(k_part)
        dk, dv = [], []
        for h, (q_aug, g_aug) in enumerate(((q0, g0), (q1, g1))):
            mine = left if h == 0 else jnp.logical_not(left)
            k_aug = jnp.where(mine, k_part, k_tail)
            v_aug = jnp.where(mine, v_part, v_tail)
            p = jnp.exp(dot_nt(k_aug, q_aug[...]))
            ds = (p * dot_nt(v_aug, g_aug[...])).astype(LOW)
            dv.append(dot_nn(p.astype(LOW), g[...]))
            dk.append(dot_nn(ds, q[...]))
            k_mine = jnp.where(mine, k_part, zero).astype(F32).T.astype(LOW)
            dq_t[...] += dot_nn(k_mine, ds)
        dk = jnp.where(left, dk[0], dk[1])
        dv = jnp.where(left, dv[0], dv[1])
        dproj[1, at, :] = dk.astype(LOW)
        dproj[2, at, :] = dv.astype(LOW)
        sums[1:2, :] += colsum(dv)
        return carry

    lax.fori_loop(0, 4, step, 0)
    dq = dq_t[...].T * HDIM ** (-0.5)
    dproj[0] = dq.astype(LOW)
    sums[0:1, :] = colsum(dq)


def ff_fwd_kernel(
    tp, tok, mixed, valid, wo_own, wo_oth, wu_own, wu_oth, wd_own, wd_oth,
    b_out, gain, bias, b_up, b_down,
    norm_two_out, normed_out, inv_out, act_out, slope_out, block_out, low_out, stats, acc,
):
    half = wo_own.shape[-1]
    ff = wu_own.shape[-1]
    wide = 512
    attn = (
        dot_nt(mixed[:, :half], flat(wo_own[:, 0, 0]))
        + dot_nt(mixed[:, half:], flat(wo_oth[:, 0, 0]))
        + b_out[...]
    )
    resid = tok[...].astype(F32) + attn
    normed, inv = norm_parts(resid)
    norm_two_out[...] = (normed * gain[...] + bias[...]).astype(LOW)
    normed_out[...] = normed.astype(LOW)
    inv_out[...] = inv
    acc[...] = jnp.zeros_like(acc)
    for side, (wu, wd) in enumerate(((wu_own, wd_own), (wu_oth, wd_oth))):

        def step(c, carry):
            at = pl.ds(pl.multiple_of(c * wide, wide), wide)
            to = pl.ds(pl.multiple_of(side * ff + c * wide, wide), wide)
            pre = dot_nn(norm_two_out[...], flat(wu[:, 0, 0, :, at])) + b_up[side : side + 1, at]
            act, slope = gelu_parts(pre)
            act = act.astype(LOW)
            if side == 0:
                act_out[:, at] = act
            slope_out[:, to] = slope.astype(LOW)
            acc[...] += dot_nt(act, flat(wd[:, 0, 0, :, at]))
            return carry

        lax.fori_loop(0, ff // wide, step, 0)
    mlp = acc[...] + b_down[...]
    block = resid + mlp
    block_out[...] = block
    low_out[...] = block.astype(LOW)

    @pl.when(pl.program_id(0) == 0)
    def _():
        stats[...] = jnp.zeros_like(stats)

    mask = valid[:, 0:1]
    stats[0:1, :] += colsum(block * block * mask)
    stats[1:2, :] += colsum(attn * attn * mask)
    stats[2:3, :] += colsum(mlp * mlp * mask)


def head_kernel(
    tp, block, lat, g_block, g_head, masks, w_mod, h1_own, h1_oth, h2_own, h2_oth,
    b_mod, b_hid1, b_hid2,
    head_out, g_lat, hid_in_out, hidden_out, branch_low_out, pre_low_out, mod_low_out, cond_out,
    dblock_out, dblock_low_out, sums_w, sums_h, sums_d,
):
    half = h1_own.shape[-1]
    valid, image = masks[:, 0:1], masks[:, 1:2]
    blk = block[...]
    sig_b = sigmoid(blk)
    cond = (blk * sig_b).astype(LOW)
    cond_out[...] = cond
    lat_in = lat[...].astype(F32)
    lat_norm, lat_inv = norm_parts(lat_in)
    shift = dot_nn(cond, flat(w_mod[:, 0])) + b_mod[0:1]
    scale = 1.0 + (dot_nn(cond, flat(w_mod[:, 1])) + b_mod[1:2])
    gate = dot_nn(cond, flat(w_mod[:, 2])) + b_mod[2:3]
    hid_in = (lat_norm * scale + shift).astype(LOW)
    hid_in_out[...] = hid_in
    branch = b_hid2[...]
    slopes = []
    for side, (h1, h2) in enumerate(((h1_own, h2_own), (h1_oth, h2_oth))):
        pre = dot_nn(hid_in, flat(h1[:, 0, 0])) + b_hid1[side : side + 1]
        sig = sigmoid(pre)
        hidden = (pre * sig).astype(LOW)
        slopes.append(sig * (1.0 + pre * (1.0 - sig)))
        if side == 0:
            hidden_out[...] = hidden
        branch = branch + dot_nt(hidden, flat(h2[:, 0, 0]))
    head_branch = gate * branch
    head_out[...] = (lat_in + head_branch).astype(LOW)
    gh = g_head[...].astype(F32) * image
    dbranch = gh * gate
    branch_low = dbranch.astype(LOW)
    branch_low_out[...] = branch_low
    dgate = gh * branch

    @pl.when(pl.program_id(0) == 0)
    def _():
        sums_w[...] = jnp.zeros_like(sums_w)
        sums_h[...] = jnp.zeros_like(sums_h)
        sums_d[...] = jnp.zeros_like(sums_d)

    dhid_in = None
    for side, (h1, h2) in enumerate(((h1_own, h2_own), (h1_oth, h2_oth))):
        dpre = dot_nn(branch_low, flat(h2[:, 0, 0])) * slopes[side]
        pre_low = dpre.astype(LOW)
        if side == 0:
            pre_low_out[...] = pre_low
            sums_h[0:1, :] += colsum(dpre)
        part = dot_nt(pre_low, flat(h1[:, 0, 0]))
        dhid_in = part if dhid_in is None else dhid_in + part
    dscale = dhid_in * lat_norm
    low0, low1, low2 = dhid_in.astype(LOW), dscale.astype(LOW), dgate.astype(LOW)
    mod_low_out[0] = low0
    mod_low_out[1] = low1
    mod_low_out[2] = low2
    sums_w[0:1, :] += colsum(dbranch)
    sums_w[1:2, :] += colsum(dhid_in)
    sums_w[2:3, :] += colsum(dscale)
    sums_w[3:4, :] += colsum(dgate)
    sums_w[4:5, :] += colsum(head_branch * head_branch * valid)
    dcond = (
        dot_nt(low0, flat(w_mod[:, 0]))
        + dot_nt(low1, flat(w_mod[:, 1]))
        + dot_nt(low2, flat(w_mod[:, 2]))
    )
    g_lat[...] = gh + norm_back(dhid_in * scale, lat_norm, lat_inv)
    dblock = g_block[...].astype(F32) * valid + dcond * (sig_b * (1.0 + blk * (1.0 - sig_b)))
    dblock_out[...] = dblock
    dblock_low_out[...] = dblock.astype(LOW)
    sums_d[0:1, :] += colsum(dblock)


def ff_bwd_kernel(
    tp, dblock, dblock_low, slope, normed_in, inv_in, wo_own, wo_oth, wu_own, wu_oth, wd_own,
    wd_oth, gain,
    dup_out, dresid_out, dresid_low_out, dmixed_out, sums_u, sums_d, acc,
):
    half = wo_own.shape[-1]
    ff = wu_own.shape[-1]
    wide = 512

    @pl.when(pl.program_id(0) == 0)
    def _():
        sums_u[...] = jnp.zeros_like(sums_u)
        sums_d[...] = jnp.zeros_like(sums_d)

    acc[...] = jnp.zeros_like(acc)
    for side, (wu, wd) in enumerate(((wu_own, wd_own), (wu_oth, wd_oth))):

        def step(c, carry):
            at = pl.ds(pl.multiple_of(c * wide, wide), wide)
            frm = pl.ds(pl.multiple_of(side * ff + c * wide, wide), wide)
            dact = dot_nn(dblock_low[...], flat(wd[:, 0, 0, :, at]))
            dpre = dact * slope[:, frm].astype(F32)
            dup = dpre.astype(LOW)
            if side == 0:
                dup_out[:, at] = dup
                sums_u[0:1, at] += colsum(dpre)
            acc[...] += dot_nt(dup, flat(wu[:, 0, 0, :, at]))
            return carry

        lax.fori_loop(0, ff // wide, step, 0)
    dnorm = acc[...]
    normed = normed_in[...].astype(F32)
    sums_d[0:1, :] += colsum(dnorm * normed)
    sums_d[1:2, :] += colsum(dnorm)
    dresid = dblock[...] + norm_back(dnorm * gain[...], normed, inv_in[...])
    sums_d[2:3, :] += colsum(dresid)
    dresid_out[...] = dresid
    low = dresid.astype(LOW)
    dresid_low_out[...] = low
    dmixed_out[:, :half] = dot_nn(low, flat(wo_own[:, 0, 0])).astype(LOW)
    dmixed_out[:, half:] = dot_nn(low, flat(wo_oth[:, 0, 0])).astype(LOW)


def tok_bwd_kernel(tp, tok, dproj, dresid, w_own, w_oth, gain, g_tok, sums):
    half = w_own.shape[-1]
    dnorm = None
    for side, w in enumerate((w_own, w_oth)):
        for t in range(3):
            part = dot_nt(dproj[t, :, side * half : (side + 1) * half], flat(w[:, 0, t]))
            dnorm = part if dnorm is None else dnorm + part
    normed, inv = norm_parts(tok[...].astype(F32))

    @pl.when(pl.program_id(0) == 0)
    def _():
        sums[...] = jnp.zeros_like(sums)

    sums[0:1, :] += colsum(dnorm * normed)
    sums[1:2, :] += colsum(dnorm)
    g_tok[...] = dresid[...] + norm_back(dnorm * gain[...], normed, inv)


def slot_masks(lengths):
    bounds = jnp.cumsum(lengths)
    positions = jnp.arange(LONG + BUF, dtype=jnp.int32)
    segment = jnp.sum((positions[:, None] >= bounds[None, :]).astype(jnp.int32), axis=1)
    starts = jnp.concatenate([jnp.zeros((1,), jnp.int32), bounds])
    first_row = jnp.sum(
        jnp.where(segment[:, None] == jnp.arange(4, dtype=jnp.int32)[None, :], starts[None, :], 0),
        axis=1,
    )
    valid_row = positions < bounds[2]
    image_row = valid_row & (positions - first_row >= BUF)
    return (segment, valid_row.astype(F32), image_row.astype(F32))


def gather(group):
    full = lax.all_gather(group, ("dp", "tp"), axis=0)
    return full.reshape(-1, 2, *group.shape)


def both_sides(mine):
    other = lax.ppermute(mine, "tp", [(0, 1), (1, 0)])
    return jnp.stack([mine, other])


def on_device(
    tokens, latents, grad_block, grad_head, image_lengths, ln1_gain, ln1_bias, w_qkv, b_qv, w_out,
    b_out, ln2_gain, ln2_bias, w_up, b_up, w_down, b_down, w_mod, b_mod, w_hid1, b_hid1, w_hid2,
    b_hid2,
):
    rows, width = tokens.shape
    head_width = latents.shape[1]
    half = w_qkv.shape[2]
    ff = w_up.shape[1]
    hid = w_hid1.shape[1]
    n_dp = width // w_out.shape[0]
    tp = lax.axis_index("tp").reshape(1)
    pairs = 2 * half // 128
    tall = rows // 2
    steps = rows // tall
    short = rows // 4
    vec = lambda v: v.reshape(1, -1)

    g_attn = gather(jnp.concatenate([w_qkv, w_out[None]]))
    g_ff = gather(jnp.stack([w_up, w_down]))
    g_mod = lax.all_gather(w_mod, "dp", axis=0)
    g_hid = gather(jnp.stack([w_hid1, w_hid2]))
    small = both_sides(jnp.concatenate([b_qv.reshape(-1), b_up, b_hid1]))
    b_qv2 = small[:, : 2 * half].reshape(2, 2, half)
    b_up2 = small[:, 2 * half : 2 * half + ff]
    b_hid2x = small[:, 2 * half + ff :]

    segment, valid_row, image_row = slot_masks(image_lengths[0])
    masks = jnp.stack([valid_row, image_row], axis=1)
    lane_of = (jnp.arange(128) % HDIM)[None, :]
    same = segment[:, None] == lane_of
    seg_q = jnp.where(same & (lane_of < 4), 1.0, 0.0).astype(LOW)
    seg_k = jnp.where(jnp.logical_not(same) & (lane_of < 4), FAR, 0.0).astype(LOW)

    norm_one, proj = run(
        qkv_kernel, tp, steps,
        [
            (tokens, row_spec(tall, width)),
            (vec(ln1_gain), const_spec(1, width)),
            (vec(ln1_bias), const_spec(1, width)),
            (g_attn, pl.BlockSpec((n_dp, 1, 3, *g_attn.shape[3:]), lambda i, tp: (0, tp[0], 0, 0, 0), pipeline_mode=pl.Buffered(1))),
            (g_attn, pl.BlockSpec((n_dp, 1, 3, *g_attn.shape[3:]), lambda i, tp: (0, 1 - tp[0], 0, 0, 0), pipeline_mode=pl.Buffered(1))),
            (b_qv2[0], const_spec(2, half)),
            (b_qv2[1], const_spec(2, half)),
        ],
        [
            (sds((rows, width), LOW), row_spec(tall, width)),
            (sds((3, rows, width), LOW), pl.BlockSpec((3, tall, width), lambda i, tp: (0, i, 0))),
        ],
        flops=2 * rows * width * 3 * width,
        nbytes=10 * rows * width,
    )

    def part_spec(t):
        return pl.BlockSpec((None, rows, 128), lambda p, tp: (t, 0, p))

    pair_spec = pl.BlockSpec((rows, 128), lambda p, tp: (0, p))
    whole = pl.BlockSpec((rows, 128), lambda p, tp: (0, 0))
    mixed, total = run(
        attn_fwd_kernel, tp, pairs,
        [
            (proj, part_spec(0)), (proj, part_spec(1)), (proj, part_spec(2)),
            (seg_q, whole), (seg_k, whole),
        ],
        [
            (sds((rows, width), LOW), pair_spec),
            (sds((rows, width), F32), pair_spec),
        ],
        flops=4 * rows * rows * 256 * 2 * pairs,
        nbytes=12 * rows * width,
        exps=2 * pairs * rows * rows,
    )

    ff_weights = [
        (g_attn, side_spec(g_attn, 1, 3, False)), (g_attn, side_spec(g_attn, 1, 3, True)),
        (g_ff, side_spec(g_ff, 1, 0, False)), (g_ff, side_spec(g_ff, 1, 0, True)),
        (g_ff, side_spec(g_ff, 1, 1, False)), (g_ff, side_spec(g_ff, 1, 1, True)),
    ]
    norm_two, normed_two, inv_two, act, slope, block, block_low, stats = run(
        ff_fwd_kernel, tp, rows // tall,
        [
            (tokens, row_spec(tall, width)), (mixed, row_spec(tall, width)),
            (masks, row_spec(tall, 2)), *ff_weights,
            (vec(b_out), const_spec(1, width)), (vec(ln2_gain), const_spec(1, width)),
            (vec(ln2_bias), const_spec(1, width)), (b_up2, const_spec(2, ff)),
            (vec(b_down), const_spec(1, width)),
        ],
        [
            (sds((rows, width), LOW), row_spec(tall, width)),
            (sds((rows, width), LOW), row_spec(tall, width)),
            (sds((rows, 1), F32), row_spec(tall, 1)),
            (sds((rows, ff), LOW), row_spec(tall, ff)),
            (sds((rows, 2 * ff), LOW), row_spec(tall, 2 * ff)),
            (sds((rows, width), F32), row_spec(tall, width)),
            (sds((rows, width), LOW), row_spec(tall, width)),
            (sds((8, width), F32), pl.BlockSpec((8, width), lambda i, tp: (0, 0))),
        ],
        scratch=[pltpu.VMEM((tall, width), F32)],
        flops=2 * rows * width * (4 * ff + width),
        nbytes=rows * (20 * width + 6 * ff) + 8 * width * ff,
        exps=4 * rows * ff,
    )

    keep = lambda n, w: (sds((n, w), F32), pl.BlockSpec((n, w), lambda i, tp: (0, 0)))
    (
        head_out, grad_latents, hid_in, hidden, branch_low, pre_low, mod_low, cond, dblock,
        dblock_low, sums_w, sums_h, sums_b,
    ) = run(
        head_kernel, tp, rows // short,
        [
            (block, row_spec(short, width)), (latents, row_spec(short, head_width)),
            (grad_block, row_spec(short, width)), (grad_head, row_spec(short, head_width)),
            (masks, row_spec(short, 2)), (g_mod, const_spec(*g_mod.shape)),
            (g_hid, side_spec(g_hid, 1, 0, False)), (g_hid, side_spec(g_hid, 1, 0, True)),
            (g_hid, side_spec(g_hid, 1, 1, False)), (g_hid, side_spec(g_hid, 1, 1, True)),
            (b_mod, const_spec(3, head_width)), (b_hid2x, const_spec(2, hid)),
            (vec(b_hid2), const_spec(1, head_width)),
        ],
        [
            (sds((rows, head_width), LOW), row_spec(short, head_width)),
            (sds((rows, head_width), F32), row_spec(short, head_width)),
            (sds((rows, head_width), LOW), row_spec(short, head_width)),
            (sds((rows, hid), LOW), row_spec(short, hid)),
            (sds((rows, head_width), LOW), row_spec(short, head_width)),
            (sds((rows, hid), LOW), row_spec(short, hid)),
            (sds((3, rows, head_width), LOW), pl.BlockSpec((3, short, head_width), lambda i, tp: (0, i, 0))),
            (sds((rows, width), LOW), row_spec(short, width)),
            (sds((rows, width), F32), row_spec(short, width)),
            (sds((rows, width), LOW), row_spec(short, width)),
            keep(8, head_width), keep(8, hid), keep(8, width),
        ],
        flops=2 * rows * head_width * (6 * width + 4 * head_width),
        nbytes=rows * (14 * width + 22 * head_width) + 20 * head_width * head_width,
        exps=rows * 2 * head_width,
    )

    dup, dresid, dresid_low, dmixed, sums_u, sums_r = run(
        ff_bwd_kernel, tp, rows // tall,
        [
            (dblock, row_spec(tall, width)), (dblock_low, row_spec(tall, width)),
            (slope, row_spec(tall, 2 * ff)), (normed_two, row_spec(tall, width)),
            (inv_two, row_spec(tall, 1)), *ff_weights, (vec(ln2_gain), const_spec(1, width)),
        ],
        [
            (sds((rows, ff), LOW), row_spec(tall, ff)),
            (sds((rows, width), F32), row_spec(tall, width)),
            (sds((rows, width), LOW), row_spec(tall, width)),
            (sds((rows, width), LOW), row_spec(tall, width)),
            keep(8, ff), keep(8, width),
        ],
        scratch=[pltpu.VMEM((tall, width), F32)],
        flops=2 * rows * width * (4 * ff + width),
        nbytes=rows * (16 * width + 6 * ff) + 8 * width * ff,
    )

    dproj, sums_qv = run(
        attn_bwd_kernel, tp, pairs,
        [
            (proj, part_spec(0)), (proj, part_spec(1)), (proj, part_spec(2)),
            (dmixed, pair_spec), (mixed, pair_spec), (total, pair_spec),
            (seg_q, whole), (seg_k, whole),
        ],
        [
            (sds((3, rows, width), LOW), pl.BlockSpec((3, rows, 128), lambda p, tp: (0, 0, p))),
            (sds((8, width), F32), pl.BlockSpec((8, 128), lambda p, tp: (0, p))),
        ],
        scratch=[pltpu.VMEM((rows, 128), LOW)] * 4 + [pltpu.VMEM((128, rows), F32)],
        flops=10 * rows * rows * 256 * 2 * pairs,
        nbytes=20 * rows * width,
        exps=2 * pairs * rows * rows,
    )
    grad_tokens, sums_t = run(
        tok_bwd_kernel, tp, steps,
        [
            (tokens, row_spec(tall, width)),
            (dproj, pl.BlockSpec((3, tall, width), lambda i, tp: (0, i, 0))),
            (dresid, row_spec(tall, width)),
            (g_attn, pl.BlockSpec((n_dp, 1, 3, *g_attn.shape[3:]), lambda i, tp: (0, tp[0], 0, 0, 0), pipeline_mode=pl.Buffered(1))),
            (g_attn, pl.BlockSpec((n_dp, 1, 3, *g_attn.shape[3:]), lambda i, tp: (0, 1 - tp[0], 0, 0, 0), pipeline_mode=pl.Buffered(1))),
            (vec(ln1_gain), const_spec(1, width)),
        ],
        [(sds((rows, width), F32), row_spec(tall, width)), keep(8, width)],
        flops=2 * rows * width * 3 * width,
        nbytes=16 * rows * width,
    )

    def scatter(parts):
        packed = [p.astype(LOW).reshape(n_dp, -1, p.shape[-1]) for p in parts]
        packed = jnp.concatenate(packed, axis=1)
        return lax.psum_scatter(packed, "dp", scatter_dimension=0, tiled=False).astype(F32)

    def by_shard(stacked):
        n, depth, cols = stacked.shape
        return jnp.transpose(stacked.reshape(n, n_dp, depth // n_dp, cols), (1, 0, 2, 3)).reshape(
            -1, cols
        )

    mod_half = head_width // 2
    mod_own = lax.dynamic_slice_in_dim(mod_low, tp[0] * mod_half, mod_half, axis=2)
    d_hid2 = dot_tn(branch_low, hidden)
    d_hid1 = dot_tn(hid_in, pre_low)
    d_mod = jnp.einsum("rd,tre->tde", cond, mod_own, preferred_element_type=F32)
    got = scatter([d_hid1, d_hid2, by_shard(d_mod.astype(LOW))])
    in_rows = head_width // n_dp
    d_w_hid1, d_w_hid2 = got[:in_rows], got[in_rows : 2 * in_rows]
    mine = got[2 * in_rows :].reshape(3, -1, mod_half)
    theirs = lax.ppermute(mine, "tp", [(0, 1), (1, 0)])
    first = tp[0] == 0
    d_w_mod = jnp.concatenate(
        [jnp.where(first, mine, theirs), jnp.where(first, theirs, mine)], axis=2
    )
    d_down = dot_tn(dblock_low, act)
    d_up = dot_tn(norm_two, dup)
    got = scatter([d_down, d_up])
    w_rows = width // n_dp
    d_w_down, d_w_up = got[:w_rows], got[w_rows:]
    d_out = dot_tn(dresid_low, mixed[:, :half])
    d_qkv = jnp.einsum("rd,tre->tde", norm_one, dproj[:, :, :half], preferred_element_type=F32)
    got = scatter([d_out, by_shard(d_qkv.astype(LOW))])
    d_w_out = got[:w_rows]
    d_w_qkv = got[w_rows:].reshape(3, w_rows, half)

    pieces = [
        sums_t[0:2].reshape(-1), sums_qv[0:2, :half].reshape(-1), sums_r[0:3].reshape(-1),
        sums_u[0], sums_b[0], sums_w[0:4].reshape(-1), sums_h[0],
    ]
    sizes = [p.shape[0] for p in pieces]
    joined = jnp.concatenate(pieces)
    joined = jnp.pad(joined, (0, -joined.shape[0] % 1024)).reshape(-1, 128)
    summed = jnp.sum(lax.all_gather(joined, "dp", axis=0), axis=0).reshape(-1)
    ends, at = [], 0
    for size in sizes:
        ends.append(summed[at : at + size])
        at += size
    ln1s, bqv, rs, d_b_up, d_b_down, ws, d_b_hid1 = ends
    ln1s, bqv, rs = ln1s.reshape(2, -1), bqv.reshape(2, -1), rs.reshape(3, -1)
    ws = ws.reshape(4, -1)

    squares = jnp.concatenate([jnp.sum(stats[0:3], axis=1), jnp.sum(sums_w[4:5], axis=1)])
    widths = jnp.array([width, width, width, head_width], F32)
    rms_values = jnp.sqrt(squares / (jnp.sum(valid_row) * widths)).reshape(1, 4)
    return (
        block_low, head_out, grad_tokens, grad_latents, ln1s[0], ln1s[1], d_w_qkv, bqv, d_w_out,
        rs[2], rs[0], rs[1], d_w_up, d_b_up, d_w_down, d_b_down, d_w_mod, ws[1:4], d_w_hid1,
        d_b_hid1, d_w_hid2, ws[0], rms_values,
    )


def solution(mesh):
    rows, one = P("dp", None), P()
    split = P("dp", "tp")
    weights = (
        one, one, P(None, "dp", "tp"), P(None, "tp"), split, one, one, one, split, P("tp"), split,
        one, P(None, "dp", None), one, split, P("tp"), split, one,
    )
    return jax.shard_map(
        on_device,
        mesh=mesh,
        in_specs=(rows, rows, rows, rows, rows) + weights,
        out_specs=(rows, rows, rows, rows) + weights + (rows,),
        check_vma=False,
    )
```

time: 1520 us -> 646 us (0.42)
  waiting for transfers between devices: 1010 us -> 299 us
  matrix products: 242 us -> 24.3 us
  Pallas kernels: 0 us -> 215 us
  blocking collectives: 92.3 us -> 22.4 us
  other arithmetic: 74.9 us -> 24.1 us
  local copies, waits for them, and re-layouts: 74.6 us -> 31.2 us
    psum x5 -> x0, waiting for transfers between devices: 262 us -> none  [the longest x1 112 us: on_device(): lax.psum(contract(hidden, wh2_full, 1, 1).astype(jnp.bfloat16), 'tp')]
    reduce_scatter x5 -> x3, waiting for transfers between devices: 347 us -> 129 us  [scatter(): lax.psum_scatter(packed, 'dp', scatter_dimension=0, tiled=False).astype(F32)]
    dot_general x63 -> x7, matrix products: 242 us -> 24.3 us  [the longest x5 13.4 us: dot_tn(): lax.dot_general(a, b, (((0,), (0,)), ((), ())), preferred_element_type=F32)]
    pallas_call x0 -> x7, Pallas kernels: none -> 215 us  [run(): pl.pallas_call(kernel, grid_spec=pltpu.PrefetchScalarGridSpec(num_scalar_...]
    unnamed x18 -> x7, waiting for transfers between devices: 209 us -> 0.62 us
    psum x1 -> x0, blocking collectives: 65.8 us -> none  [on_device(): lax.psum((d_ln1_gain, d_ln1_bias, d_b_qv, d_b_out, d_ln2_gain, d_ln2_bias...]
    reduce_sum x20 -> x4, other arithmetic: 42.6 us -> 2.02 us  [the longest x1 1.25 us: on_device(): rms_values = jnp.sqrt(squares / (jnp.sum(valid_row) * widths)).reshape(1, 4)]
    all_gather x6 -> x4, waiting for transfers between devices: 190 us -> 167 us  [the longest x3 113 us: gather(): full = lax.all_gather(group, ('dp', 'tp'), axis=0)]
  transfers between devices with their start and end apart: 17 -> 9, of which waited for: 16 -> 7; matrix products, arithmetic and copies ran while one was open for 10% -> 10% of each run, Pallas kernels for 0% -> 15%
where the time goes in v1:
time: 646 us; the launch traced here: 636 us
  waiting for transfers between devices  299 us (46%)
  Pallas kernels  215 us (33%)
  local copies, waits for them, and re-layouts  31.2 us (5%)
  matrix products  24.3 us (4%)
  other arithmetic  24.1 us (4%)
  blocking collectives  22.4 us (3%)
  between operations  15 us (2%)
    pallas_call x7, Pallas kernels, run(): pl.pallas_call(kernel, grid_spec=pltpu.PrefetchScalarGridSpec(num_scalar_...  215 us
    reduce_scatter x3, waiting for transfers between devices, scatter(): lax.psum_scatter(packed, 'dp', scatter_dimension=0, tiled=False).astype(F32)  129 us
    all_gather x3, waiting for transfers between devices, gather(): full = lax.all_gather(group, ('dp', 'tp'), axis=0)  113 us
    all_gather x1, waiting for transfers between devices, on_device(): g_mod = lax.all_gather(w_mod, 'dp', axis=0)  54.1 us
    all_gather x1, blocking collectives, on_device(): summed = jnp.sum(lax.all_gather(joined, 'dp', axis=0), axis=0).reshape(-1)  22.4 us
    dot_general x5, matrix products, dot_tn(): lax.dot_general(a, b, (((0,), (0,)), ((), ())), preferred_element_type=F32)  13.4 us
  transfers between devices with their start and end apart: 9, of which 7 were waited for; matrix products, arithmetic and copies ran while one was open for 10% of the time, Pallas kernels for 15%

profile of v1, /device:TPU:0, one launch (start us, length us, event | category | flops | bytes accessed | tf_op | source)
XLA Modules:
  0.0 636.2 jit_solution(12341260174835818419)
XLA Ops:
  7.3 1.6 pad_maximum_fusion.5
  9.0 1.7 pad_maximum_fusion.4
  10.8 1.5 pad_maximum_fusion.6
  15.1 2.9 collective-permute-start
  28.6 49.4 %all-gather.9.cloned.1.call-done = bf16[128,48,384]{2,1,0:T(8,128)(2,1)} async-done(((bf16[4,48,384]{2,1,0:T(8,128)(2,1)}), bf16[128,48,384]{2,1,0:T(8,128)(2,1)}) %all-gather.9.cloned.1.call-update) | async-done | bytes 4718608 | tf_op jit(solution)/shard_map/all_gather | solution.py:430
  77.9 10.2 %shard_map.407 = (bf16[1088,768]{1,0:T(8,128)(2,1)}, bf16[3,1088,768]{2,1,0:T(8,128)(2,1)}) custom-call(s32[1]{0:T(128)} %bitcast.tp, bf16[1088,768]{1,0:T(8,128)(2,1)} %tok.5, f32[1,768]{1,0:T(1,128)} %reshape.230.gain, f32[1,768]{1,0:T(1,128)} %reshape.231.bias, bf16[16,2,4,48,384]{4,3,2,1,0:T(8,128)(2,1)} %bitcast.94, ...), custom_call_target="tpu_custom_call" | custom-call | flops 3850371072 | bytes 8355840 | tf_op jit(solution)/shard_map/pallas_call | solution.py:117
  88.1 38.7 %shard_map.408 = (bf16[1088,768]{1,0:T(8,128)(2,1)}, f32[1088,768]{1,0:T(8,128)}) custom-call(s32[1]{0:T(128)} %bitcast.tp, bf16[3,1088,768]{2,1,0:T(8,128)(2,1)} %get-tuple-element.58.q.k.v, bf16[3,1088,768]{2,1,0:T(8,128)(2,1)} %get-tuple-element.58.q.k.v, bf16[3,1088,768]{2,1,0:T(8,128)(2,1)} %get-tuple-element.58.q.k.v, ...), custom_call_target="tpu_custom_call" | custom-call | flops 14545846272 | bytes 10027008 | tf_op jit(solution)/shard_map/pallas_call | solution.py:117
  126.8 35.5 %all-gather.11.cloned.1.call-done = bf16[64,48,1536]{2,1,0:T(8,128)(2,1)} async-done(((bf16[2,48,1536]{2,1,0:T(8,128)(2,1)}), bf16[64,48,1536]{2,1,0:T(8,128)(2,1)}) %all-gather.11.cloned.1.call-update) | async-done | bytes 9437200 | tf_op jit(solution)/shard_map/all_gather | solution.py:430
  162.3 35.9 %shard_map.409 = (bf16[1088,768]{1,0:T(8,128)(2,1)}, bf16[1088,768]{1,0:T(8,128)(2,1)}, f32[1088,1]{1,0:T(8,128)}, bf16[1088,1536]{1,0:T(8,128)(2,1)}, bf16[1088...) custom-call(s32[1]{0:T(128)} %bitcast.tp, bf16[1088,768]{1,0:T(8,128)(2,1)} %tok.5, ...), custom_call_target="tpu_custom_call" | custom-call | flops 11551113216 | bytes 36175872 | tf_op jit(solution)/shard_map/pallas_call | solution.py:117
  198.2 28.4 %all-gather.15.cloned.1.call-done = bf16[64,64,512]{2,1,0:T(8,128)(2,1)} async-done(((bf16[2,64,512]{2,1,0:T(8,128)(2,1)}), bf16[64,64,512]{2,1,0:T(8,128)(2,1)}) %all-gather.15.cloned.1.call-update) | async-done | bytes 4194320 | tf_op jit(solution)/shard_map/all_gather | solution.py:430
  226.6 54.1 %all-gather.13.cloned.1.call-done = bf16[48,48,1024]{2,1,0:T(8,128)(2,1)} async-done(((bf16[3,48,1024]{2,1,0:T(8,128)(2,1)}), bf16[48,48,1024]{2,1,0:T(8,128)(2,1)}) %all-gather.13.cloned.1.call-update) | async-done | bytes 4718608 | tf_op jit(solution)/shard_map/all_gather | solution.py:459
  280.7 36.1 %shard_map.410 = (bf16[1088,1024]{1,0:T(8,128)(2,1)}, f32[1088,1024]{1,0:T(8,128)}, bf16[1088,1024]{1,0:T(8,128)(2,1)}, bf16[1088,512]{1,0:T(8,128)(2,1)}, bf16[...) custom-call(s32[1]{0:T(128)} %bitcast.tp, ...), custom_call_target="tpu_custom_call" | custom-call | flops 19394461696 | bytes 57180160 | tf_op jit(solution)/shard_map/pallas_call | solution.py:117
  316.8 25.8 %shard_map.411 = (bf16[1088,1536]{1,0:T(8,128)(2,1)}, f32[1088,768]{1,0:T(8,128)}, bf16[1088,768]{1,0:T(8,128)(2,1)}, bf16[1088,768]{1,0:T(8,128)(2,1)}, f32[8,1536]{1,0:T(8,128)}, /*index=5*/f32[8,768]{1,0:T(8,128)}) custom-call(s32[1]{0:T(128)} %bitcast.tp, f32[1088,768]{1,0:T(8,128)} %get-tuple-element.63.dblock, ...), custom_call_target="tpu_custom_call" | custom-call | flops 11551113216 | bytes 32833536 | tf_op jit(solution)/shard_map/pallas_call | solution.py:117
  342.6 56.1 %shard_map.412 = (bf16[3,1088,768]{2,1,0:T(8,128)(2,1)}, f32[8,768]{1,0:T(8,128)}) custom-call(s32[1]{0:T(128)} %bitcast.tp, bf16[3,1088,768]{2,1,0:T(8,128)(2,1)} %get-tuple-element.58.q.k.v, bf16[3,1088,768]{2,1,0:T(8,128)(2,1)} %get-tuple-element.58.q.k.v, bf16[3,1088,768]{2,1,0:T(8,128)(2,1)} %get-tuple-element.58.q.k.v, ...), custom_call_target="tpu_custom_call" | custom-call | flops 36364615680 | bytes 16711680 | tf_op jit(solution)/shard_map/pallas_call | solution.py:117
  398.7 4.2 convert_bitcast_fusion.1
  407.2 1.8 pad_maximum_fusion.2
  410.4 6.6 %convert_bitcast_fusion = bf16[3,768,512]{1,2,0:T(8,128)(2,1)} fusion(bf16[3,1088,1024]{2,1,0:T(8,128)(2,1)} %get-tuple-element.90, s32[]{:T(128)S(6)} %select_n.49, bf16[1088,768]{1,0:T(8,128)(2,1)S(1)} %copy-done.20), kind=kOutput, calls=%fused_computation.9 | convolution fusion | flops 2568093696 | bytes 7372804 | tf_op jit(solution)/shard_map/rd,tre->tde/dot_general | solution.py:640
  417.1 3.1 copy.65
  422.2 1.6 convolution_convert_fusion.3
  424.2 1.5 convolution_convert_fusion.2
  425.8 2.3 pad_maximum_fusion.1
  429.5 5.6 convolution_convert_fusion.1
  435.1 3.6 convolution_convert_fusion
  438.7 2.5 pad_maximum_fusion
  442.5 12.4 %shard_map.413 = (f32[1088,768]{1,0:T(8,128)}, f32[8,768]{1,0:T(8,128)}) custom-call(s32[1]{0:T(128)} %bitcast.tp, bf16[1088,768]{1,0:T(8,128)(2,1)} %tok.5, bf16[3,1088,768]{2,1,0:T(8,128)(2,1)} %get-tuple-element.70.dproj, f32[1088,768]{1,0:T(8,128)} %get-tuple-element.71.dresid, bf16[16,2,4,48,384]{4,3,2,1,0:T(8,128)(2,1)} %bitcast.100, ...), custom_call_target="tpu_custom_call" | custom-call | flops 3850371072 | bytes 13369344 | tf_op jit(solution)/shard_map/pallas_call | solution.py:117
  458.8 22.4 %all_gather.35 = f32[16,96,128]{2,1,0:T(8,128)S(1)} all-gather(f32[1,96,128]{2,1,0:T(8,128)S(1)} %pad_bitcast_fusion), channel_id=1, replica_groups=mesh['dp'=16,'tp'=2] {'dp'}, dimensions={0}, use_global_device_ids=true | all-gather | bytes 835584 | tf_op jit(solution)/shard_map/all_gather | solution.py:668
  483.8 1.9 sqrt_bitcast_fusion
  488.5 60.1 %reduce-scatter.8.cloned.1.call-done = bf16[1,272,512]{2,1,0:T(8,128)(2,1)} async-done(((bf16[16,272,512]{2,1,0:T(8,128)(2,1)}), bf16[1,272,512]{2,1,0:T(8,128)(2,1)}) %reduce-scatter.8.cloned.1.call-update) | async-done | bytes 278544 | tf_op jit(solution)/shard_map/reduce_scatter | solution.py:628
  549.5 1.6 collective-permute-start.1
  551.7 1.6 slice.208
  555.0 2.3 collective-permute-done.1
  558.2 68.9 %reduce-scatter.6.cloned.1.call-done = bf16[1,96,1536]{2,1,0:T(8,128)(2,1)} async-done(((bf16[16,96,1536]{2,1,0:T(8,128)(2,1)}), bf16[1,96,1536]{2,1,0:T(8,128)(2,1)}) %reduce-scatter.6.cloned.1.call-update) | async-done | bytes 294928 | tf_op jit(solution)/shard_map/reduce_scatter | solution.py:628
  (132 shorter events, 39.4 us)
Async XLA Ops:
  7.2 14.9 %copy-start.5 = (f32[768]{0:T(1024)S(1)}, f32[768]{0:T(1024)}, u32[]{:S(2)}) copy-start(f32[768]{0:T(1024)} %param.29) | copy-start | bytes 9220
  7.2 15.5 %copy-start.6 = (f32[768]{0:T(1024)S(1)}, f32[768]{0:T(1024)}, u32[]{:S(2)}) copy-start(f32[768]{0:T(1024)} %param.30) | copy-start | bytes 9220
  7.2 17.2 %copy-start.7 = (f32[768]{0:T(1024)S(1)}, f32[768]{0:T(1024)}, u32[]{:S(2)}) copy-start(f32[768]{0:T(1024)} %param.35) | copy-start | bytes 9220
  7.2 17.8 %copy-start.8 = (f32[768]{0:T(1024)S(1)}, f32[768]{0:T(1024)}, u32[]{:S(2)}) copy-start(f32[768]{0:T(1024)} %param.34) | copy-start | bytes 9220
  7.2 18.3 %copy-start.9 = (f32[768]{0:T(1024)S(1)}, f32[768]{0:T(1024)}, u32[]{:S(2)}) copy-start(f32[768]{0:T(1024)} %param.36) | copy-start | bytes 9220
  7.2 18.9 %copy-start.10 = (f32[768]{0:T(1024)S(1)}, f32[768]{0:T(1024)}, u32[]{:S(2)}) copy-start(f32[768]{0:T(1024)} %param.40) | copy-start | bytes 9220
  7.3 70.7 %all-gather.9.cloned.1.call-start = ((), (), s32[]{:S(2)}) async-start(), calls=%async_computation.6 | async-start | bytes 4866048 | tf_op jit(solution)/shard_map/all_gather | solution.py:430
  8.9 153.4 %all-gather.11.cloned.1.call-start = ((), (), s32[]{:S(2)}) async-start(), calls=%async_computation.7 | async-start | bytes 9732096 | tf_op jit(solution)/shard_map/all_gather | solution.py:430
  10.7 215.9 %all-gather.15.cloned.1.call-start = ((), (), s32[]{:S(2)}) async-start(), calls=%async_computation.9 | async-start | bytes 4325376 | tf_op jit(solution)/shard_map/all_gather | solution.py:430
  12.3 268.4 %all-gather.13.cloned.1.call-start = ((), (), s32[]{:S(2)}) async-start(), calls=%async_computation.8 | async-start | bytes 5013504 | tf_op jit(solution)/shard_map/all_gather | solution.py:459
  12.9 474.6 %reduce-scatter.4.cloned.1.call-start = ((), (), s32[]{:S(2)}) async-start(), calls=%async_computation.3 | async-start | bytes 2506752 | tf_op jit(solution)/shard_map/reduce_scatter | solution.py:628
  15.1 11.7 %collective-permute-start = (f32[2816]{0:T(1024)S(1)}, f32[2816]{0:T(1024)S(1)}, u32[]{:S(2)}, u32[]{:S(2)}) collective-permute-start(f32[2816]{0:T(1024)S(1)} %constant_dynamic-update-slice_fusion), channel_id=1, source_target_pairs={{0,1},{1,0},{2,3},{3,2},{4,5},{5,4},{6,7},{7,6},{8,9},{9,8},{10,11... | collective-permute-start | bytes 33800 | tf_op jit(solution)/shard_map/ppermute | solution.py:435
  342.6 56.1 %copy-start.17 = (bf16[1088,768]{1,0:T(8,128)(2,1)S(1)}, bf16[1088,768]{1,0:T(8,128)(2,1)}, u32[]{:S(2)}) copy-start(bf16[1088,768]{1,0:T(8,128)(2,1)} %get-tuple-element.82) | copy-start | bytes 5013508
  404.0 1.4 copy-start
  404.1 1.9 copy-start.14
  409.0 1.4 copy-start.20
  409.0 139.5 %reduce-scatter.8.cloned.1.call-start = ((), (), s32[]{:S(2)}) async-start(), calls=%async_computation.5 | async-start | bytes 4734976 | tf_op jit(solution)/shard_map/reduce_scatter | solution.py:628
  420.2 1.7 copy-start.16
  420.2 2.0 copy-start.19
  422.2 1.7 copy-start.15
  422.2 2.0 copy-start.18
  428.1 1.4 copy-start.1
  428.1 198.9 %reduce-scatter.6.cloned.1.call-start = ((), (), s32[]{:S(2)}) async-start(), calls=%async_computation.4 | async-start | bytes 5013504 | tf_op jit(solution)/shard_map/reduce_scatter | solution.py:628
  429.5 5.6 copy-start.12
  429.5 5.6 copy-start.13
  442.5 13.9 %copy-start.4 = (f32[8,768]{1,0:T(8,128)S(1)}, f32[8,768]{1,0:T(8,128)}, u32[]{:S(2)}) copy-start(f32[8,768]{1,0:T(8,128)} %get-tuple-element.76) | copy-start | bytes 73732
  442.5 16.3 %copy-start.2 = (f32[8,1024]{1,0:T(8,128)S(1)}, f32[8,1024]{1,0:T(8,128)}, u32[]{:S(2)}) copy-start(f32[8,1024]{1,0:T(8,128)} %get-tuple-element.79) | copy-start | bytes 98308
  442.5 40.6 %copy-start.3 = (f32[8,768]{1,0:T(8,128)S(1)}, f32[8,768]{1,0:T(8,128)}, u32[]{:S(2)}) copy-start(f32[8,768]{1,0:T(8,128)} %get-tuple-element.92) | copy-start | bytes 73732
  442.5 41.4 %copy-start.11 = (f32[4]{0:T(128)S(1)}, f32[4]{0:T(128)}, u32[]{:S(2)}) copy-start(f32[4]{0:T(128)} %constant.42.clone) | copy-start | bytes 52
  549.5 7.8 %collective-permute-start.1 = (f32[3,48,512]{2,1,0:T(8,128)S(1)}, f32[3,48,512]{2,1,0:T(8,128)S(1)}, u32[]{:S(2)}, u32[]{:S(2)}) collective-permute-start(f32[3,48,512]{2,1,0:T(8,128)S(1)} %bitcast.108), channel_id=1, source_target_pairs={{0,1},{1,0},{2,3},{3,2},{4,5},{5,4},{6,7},{7,6},{8,9},{9,8},{10,11... | collective-permute-start | bytes 884744 | tf_op jit(solution)/shard_map/ppermute | solution.py:645
Sparse Core Ops, SparseCore 0:
  11.6 66.3 all-gather.8
  81.4 80.8 all-gather.10
  165.9 60.6 all-gather.14
  228.7 51.9 all-gather.12
  409.1 61.5 reduce-scatter.3
  475.0 73.4 reduce-scatter.7
  552.4 74.6 reduce-scatter.5

commit v2 on v1

v2 whole, which is shorter than its diff:
```python
import jax
import jax.numpy as jnp
from jax import lax
from jax.experimental import pallas as pl
from jax.experimental.pallas import tpu as pltpu
from jax.sharding import PartitionSpec as P

HDIM = 64
BUF = 64
LONG = 1024
EPS_NORM = 1e-06
FAR = -1e30
VMEM_LIMIT = 60 * 1024 * 1024
F32 = jnp.float32
LOW = jnp.bfloat16


def params():
    return pltpu.CompilerParams(vmem_limit_bytes=VMEM_LIMIT)


def dot_nn(a, b):
    return lax.dot_general(a, b, (((1,), (0,)), ((), ())), preferred_element_type=F32)


def dot_nt(a, b):
    return lax.dot_general(a, b, (((1,), (1,)), ((), ())), preferred_element_type=F32)


def dot_tn(a, b):
    return lax.dot_general(a, b, (((0,), (0,)), ((), ())), preferred_element_type=F32)


def norm_parts(values):
    row_mean = jnp.mean(values, axis=-1, keepdims=True)
    centred = values - row_mean
    inv_dev = lax.rsqrt(jnp.mean(centred * centred, axis=-1, keepdims=True) + EPS_NORM)
    return centred * inv_dev, inv_dev


def norm_back(grad_norm, normed, inv_dev):
    mean_grad = jnp.mean(grad_norm, axis=-1, keepdims=True)
    mean_cross = jnp.mean(grad_norm * normed, axis=-1, keepdims=True)
    return inv_dev * (grad_norm - mean_grad - normed * mean_cross)


TANH_POLY = (
    1.75632313e-09, -1.32267789e-07, 3.96479041e-06, -5.53064013e-05, -3.25945666e-05,
    3.63330843e-02, 7.97884942e-01,
)


def gelu_parts(x):
    u = x * x
    poly = TANH_POLY[0]
    for term in TANH_POLY[1:]:
        poly = poly * u + term
    cdf = 0.5 * jnp.tanh(x * poly) + 0.5
    bell = jnp.exp2(u * -0.7213475204444817)
    return x * cdf, cdf + (x * 0.3989422804014327) * bell


def sigmoid(x):
    return 0.5 * jnp.tanh(0.5 * x) + 0.5


def flat(block):
    rows = 1
    for size in block.shape[:-1]:
        rows *= size
    return block.reshape(rows, block.shape[-1])


def colsum(values):
    return jnp.sum(values, axis=0, keepdims=True)


SHARDS = 16
TP, CORE, ENDS = 0, 1, 2


def row_spec(rows, *tail):
    zeros = (0,) * len(tail)
    return pl.BlockSpec((rows, *tail), lambda i, meta: (i, *zeros))


def const_spec(*shape):
    zeros = (0,) * len(shape)
    return pl.BlockSpec(shape, lambda i, meta: zeros, pipeline_mode=pl.Buffered(1))


def sum_spec(rows, cols):
    return pl.BlockSpec((rows, cols), lambda i, meta: (0, 0))


ANY = pl.BlockSpec(memory_space=pl.ANY)


def sds(shape, dtype):
    return jax.ShapeDtypeStruct(shape, dtype)


def run(kernel, meta, steps, ins, outs, scratch=(), flops=0, nbytes=0, exps=0):
    return pl.pallas_call(
        kernel,
        grid_spec=pltpu.PrefetchScalarGridSpec(
            num_scalar_prefetch=1,
            grid=(steps,),
            in_specs=[spec for _, spec in ins],
            out_specs=[spec for _, spec in outs],
            scratch_shapes=list(scratch),
        ),
        out_shape=[shape for shape, _ in outs],
        compiler_params=params(),
        cost_estimate=pl.CostEstimate(flops=flops, bytes_accessed=nbytes, transcendentals=exps),
    )(meta, *[arr for arr, _ in ins])


def fetch(meta, pair, at, count, into, sems):
    core = meta[CORE]
    return [
        pltpu.make_async_copy(ref.at[:, at : at + count, :], into.at[:, side], sems.at[i])
        for i, (ref, side) in enumerate(zip(pair, (core, 1 - core)))
    ]


def in_first_step(copies, act):
    @pl.when(pl.program_id(0) == 0)
    def _():
        for copy in copies:
            getattr(copy, act)()


def row_masks(meta, rows):
    at = pl.program_id(0) * rows + lax.broadcasted_iota(jnp.int32, (rows, 1), 0)
    e0, e1, e2 = meta[ENDS], meta[ENDS + 1], meta[ENDS + 2]
    first = jnp.where(at < e0, 0, jnp.where(at < e1, e0, jnp.where(at < e2, e1, e2)))
    valid = at < e2
    image = valid & (at - first >= BUF)
    return jnp.where(valid, 1.0, 0.0), jnp.where(image, 1.0, 0.0)


def project(norm_one, w, bias, proj_out):
    half = w.shape[-1]
    rows = w.shape[2] // 3
    for t in range(3):
        proj = dot_nn(norm_one, flat(w[:, :, t * rows : (t + 1) * rows, :]))
        if t == 0:
            low = ((proj + bias[0:1, :half]).astype(LOW).astype(F32) * HDIM ** (-0.5)).astype(LOW)
        elif t == 1:
            low = proj.astype(LOW)
        else:
            low = (proj + bias[1:2, :half]).astype(LOW)
        proj_out[t] = low


def qkv_own_kernel(meta, tok, vecs, w0, w1, b_qv, norm_out, proj_out, w, sems):
    copies = fetch(meta, (w0, w1), 0, w.shape[2], w, sems)
    in_first_step(copies, "start")
    normed, _ = norm_parts(tok[...].astype(F32))
    norm_one = (normed * vecs[0:1] + vecs[1:2]).astype(LOW)
    norm_out[...] = norm_one
    in_first_step(copies, "wait")
    project(norm_one, w, b_qv, proj_out)


def qkv_other_kernel(meta, norm_one, w0, w1, b_qv, proj_out, w, sems):
    copies = fetch(meta, (w0, w1), 0, w.shape[2], w, sems)
    in_first_step(copies, "start")
    in_first_step(copies, "wait")
    project(norm_one[...], w, b_qv, proj_out)


def lanes():
    return lax.broadcasted_iota(jnp.int32, (1, 128), 1)


def attn_fwd_kernel(meta, q, k, v, seg_q, seg_k, mixed, total):
    rows = q.shape[0]
    chunk = rows // 4
    left = lanes() < HDIM
    k_all, v_all = k[...], v[...]
    one = jnp.ones_like(v_all)
    k_aug = (jnp.where(left, k_all, seg_k[...]), jnp.where(left, seg_k[...], k_all))
    v_aug = (jnp.where(left, v_all, one), jnp.where(left, one, v_all))

    def step(i, carry):
        at = pl.ds(pl.multiple_of(i * chunk, 16), chunk)
        q_part, seg_part = q[at, :], seg_q[at, :]
        q_aug = (jnp.where(left, q_part, seg_part), jnp.where(left, seg_part, q_part))
        outs = []
        for h in range(2):
            s = dot_nt(q_aug[h], k_aug[h])
            top = jnp.max(s, axis=1, keepdims=True)
            p = jnp.exp(s - top).astype(LOW)
            outs.append((dot_nn(p, v_aug[h]), top))
        mix = jnp.where(left, outs[0][0], outs[1][0])
        tot = jnp.where(left, outs[1][0], outs[0][0])
        tot = pltpu.roll(tot, HDIM, 1)
        mixed[at, :] = (mix / tot).astype(LOW)
        total[at, :] = jnp.where(left, outs[0][1], outs[1][1]) + jnp.log(tot)
        return carry

    lax.fori_loop(0, 4, step, 0, unroll=True)


def three_terms(value, at, base):
    lane = lanes() & (HDIM - 1)
    hi = value.astype(LOW)
    rest = value - hi.astype(F32)
    mid = rest.astype(LOW)
    low = (rest - mid.astype(F32)).astype(LOW)
    out = jnp.where(lane == at, hi, base)
    out = jnp.where(lane == at + 1, mid, out)
    return jnp.where(lane == at + 2, low, out)


def attn_bwd_kernel(meta, q, k, v, g, mixed, total, seg_q, seg_k, dproj, sums):
    left = lanes() < HDIM
    lane = lanes() & (HDIM - 1)
    q_all, k_all, v_all, g_all = q[...], k[...], v[...], g[...]
    cross = g_all.astype(F32) * mixed[...].astype(F32)
    d_left = jnp.sum(jnp.where(left, cross, 0.0), axis=1, keepdims=True)
    d_right = jnp.sum(jnp.where(left, 0.0, cross), axis=1, keepdims=True)
    q_tail = three_terms(-pltpu.roll(total[...], HDIM, 1), 4, seg_q[...])
    g_tail = three_terms(jnp.where(left, -d_right, -d_left), 0, jnp.zeros_like(g_all))
    k_tail = seg_k[...] + jnp.where((lane >= 4) & (lane < 7), 1.0, 0.0).astype(LOW)
    v_tail = jnp.broadcast_to(jnp.where(lane < 3, 1.0, 0.0).astype(LOW), v_all.shape)
    zero = jnp.zeros_like(k_all)
    dk, dv, dq_t = [], [], None
    for h in range(2):
        mine = left if h == 0 else jnp.logical_not(left)
        p = jnp.exp(dot_nt(jnp.where(mine, k_all, k_tail), jnp.where(mine, q_all, q_tail)))
        dp = dot_nt(jnp.where(mine, v_all, v_tail), jnp.where(mine, g_all, g_tail))
        ds = (p * dp).astype(LOW)
        dv.append(dot_nn(p.astype(LOW), g_all))
        dk.append(dot_nn(ds, q_all))
        part = dot_nn(jnp.where(mine, k_all, zero).astype(F32).T.astype(LOW), ds)
        dq_t = part if dq_t is None else dq_t + part
    dk = jnp.where(left, dk[0], dk[1])
    dv = jnp.where(left, dv[0], dv[1])
    dq = dq_t.T * HDIM ** (-0.5)
    dproj[0] = dq.astype(LOW)
    dproj[1] = dk.astype(LOW)
    dproj[2] = dv.astype(LOW)
    sums[0:1, :] = colsum(dq)
    sums[1:2, :] = colsum(dv)


def ff_fwd_kernel(
    meta, tok, mixed_own, mixed_oth, own0, own1, oth0, oth1, w_ff, vecs, b_up,
    norm_two_out, normed_out, inv_out, act_out, slope_out, block_out, low_out, stats,
    wo_own, wo_oth, sems_own, sems_oth,
):
    out_rows = wo_own.shape[2]
    copies = fetch(meta, (own0, own1), 3 * out_rows, out_rows, wo_own, sems_own)
    copies += fetch(meta, (oth0, oth1), 3 * out_rows, out_rows, wo_oth, sems_oth)
    in_first_step(copies, "start")
    in_first_step(copies, "wait")
    attn = (
        dot_nt(mixed_own[...], flat(wo_own[...]))
        + dot_nt(mixed_oth[...], flat(wo_oth[...]))
        + vecs[2:3]
    )
    resid = tok[...].astype(F32) + attn
    normed, inv = norm_parts(resid)
    norm_two = (normed * vecs[3:4] + vecs[4:5]).astype(LOW)
    norm_two_out[...] = norm_two
    normed_out[...] = normed.astype(LOW)
    inv_out[...] = jnp.broadcast_to(inv, inv_out.shape)
    wide = w_ff.shape[-1]
    ff = act_out.shape[-1]
    parts = ff // wide
    tall = w_ff.shape[2] // (2 * parts)
    mlp = vecs[5:6]
    before = None
    for n in range(2 * parts + 1):
        if n < 2 * parts:
            side, c = divmod(n, parts)
            at_side = meta[TP] if side == 0 else 1 - meta[TP]
            at = slice(c * wide, (c + 1) * wide)
            pre = dot_nn(norm_two, flat(w_ff[:, at_side, c * tall : (c + 1) * tall, :]))
            pre = pre + b_up[side : side + 1, at]
        if before is not None:
            act, side_b, c_b = before
            down = slice((parts + c_b) * tall, (parts + c_b + 1) * tall)
            mlp = mlp + dot_nt(act, flat(w_ff[:, side_b, down, :]))
        if n < 2 * parts:
            act, slope = gelu_parts(pre)
            act = act.astype(LOW)
            if side == 0:
                act_out[:, at] = act
            slope_out[:, side * ff + c * wide : side * ff + (c + 1) * wide] = slope.astype(LOW)
            before = (act, at_side, c)
    block = resid + mlp
    block_out[...] = block
    low_out[...] = block.astype(LOW)

    @pl.when(pl.program_id(0) == 0)
    def _():
        stats[...] = jnp.zeros_like(stats)

    valid, _ = row_masks(meta, block.shape[0])
    stats[0:1, :] += colsum(block * block * valid)
    stats[1:2, :] += colsum(attn * attn * valid)
    stats[2:3, :] += colsum(mlp * mlp * valid)


def head_kernel(
    meta, block, lat, g_block, g_head, own0, own1, oth0, oth1, b_mod, b_hid1, b_hid2,
    head_out, g_lat, hid_in_out, hidden_out, branch_low_out, pre_low_out, mod_low_out, cond_out,
    dblock_out, dblock_low_out, sums_w, sums_h, sums_d,
    w_own, w_oth, sems_own, sems_oth,
):
    copies = fetch(meta, (own0, own1), 0, w_own.shape[2], w_own, sems_own)
    copies += fetch(meta, (oth0, oth1), 0, w_oth.shape[2], w_oth, sems_oth)
    in_first_step(copies, "start")
    half = hidden_out.shape[-1]
    in_rows = 2 * half // SHARDS
    mod_rows = block.shape[-1] // SHARDS

    def hid(which, side):
        w = w_own if side == 0 else w_oth
        return flat(w[:, :, which * in_rows : (which + 1) * in_rows, :])

    def mod(t, side):
        at = 2 * in_rows + (2 * t + side) * mod_rows
        return flat(w_own[:, :, at : at + mod_rows, :])

    def modulation(t):
        parts = [dot_nn(cond, mod(t, side)) for side in range(2)]
        return jnp.concatenate(parts, axis=1) + b_mod[t : t + 1]

    valid, image = row_masks(meta, block.shape[0])
    blk = block[...]
    sig_b = sigmoid(blk)
    cond = (blk * sig_b).astype(LOW)
    cond_out[...] = cond
    lat_in = lat[...].astype(F32)
    lat_norm, lat_inv = norm_parts(lat_in)
    in_first_step(copies, "wait")
    shift = modulation(0)
    scale = 1.0 + modulation(1)
    gate = modulation(2)
    hid_in = (lat_norm * scale + shift).astype(LOW)
    hid_in_out[...] = hid_in
    branch = b_hid2[...]
    slopes = []
    for side in range(2):
        pre = dot_nn(hid_in, hid(0, side)) + b_hid1[side : side + 1]
        sig = sigmoid(pre)
        hidden = (pre * sig).astype(LOW)
        slopes.append(sig * (1.0 + pre * (1.0 - sig)))
        if side == 0:
            hidden_out[...] = hidden
        branch = branch + dot_nt(hidden, hid(1, side))
    head_branch = gate * branch
    head_out[...] = (lat_in + head_branch).astype(LOW)
    gh = g_head[...].astype(F32) * image
    dbranch = gh * gate
    branch_low = dbranch.astype(LOW)
    branch_low_out[...] = branch_low
    dgate = gh * branch

    @pl.when(pl.program_id(0) == 0)
    def _():
        sums_w[...] = jnp.zeros_like(sums_w)
        sums_h[...] = jnp.zeros_like(sums_h)
        sums_d[...] = jnp.zeros_like(sums_d)

    dhid_in = None
    for side in range(2):
        dpre = dot_nn(branch_low, hid(1, side)) * slopes[side]
        pre_low = dpre.astype(LOW)
        if side == 0:
            pre_low_out[...] = pre_low
            sums_h[0:1, :] += colsum(dpre)
        part = dot_nt(pre_low, hid(0, side))
        dhid_in = part if dhid_in is None else dhid_in + part
    dscale = dhid_in * lat_norm
    lows = [dhid_in.astype(LOW), dscale.astype(LOW), dgate.astype(LOW)]
    dcond = None
    for t in range(3):
        mod_low_out[t] = jnp.where(meta[TP] == 0, lows[t][:, :half], lows[t][:, half:])
        for side in range(2):
            part = dot_nt(lows[t][:, side * half : (side + 1) * half], mod(t, side))
            dcond = part if dcond is None else dcond + part
    sums_w[0:1, :] += colsum(dbranch)
    sums_w[1:2, :] += colsum(dhid_in)
    sums_w[2:3, :] += colsum(dscale)
    sums_w[3:4, :] += colsum(dgate)
    sums_w[4:5, :] += colsum(head_branch * head_branch * valid)
    g_lat[...] = gh + norm_back(dhid_in * scale, lat_norm, lat_inv)
    dblock = g_block[...].astype(F32) * valid + dcond * (sig_b * (1.0 + blk * (1.0 - sig_b)))
    dblock_out[...] = dblock
    dblock_low_out[...] = dblock.astype(LOW)
    sums_d[0:1, :] += colsum(dblock)


def ff_bwd_kernel(
    meta, dblock, dblock_low, slope, normed_in, inv_in, own0, own1, oth0, oth1, w_ff, vecs,
    dup_out, dresid_out, dresid_low_out, dmixed_own_out, dmixed_oth_out, sums_u, sums_d,
    wo_own, wo_oth, sems_own, sems_oth,
):
    out_rows = wo_own.shape[2]
    copies = fetch(meta, (own0, own1), 3 * out_rows, out_rows, wo_own, sems_own)
    copies += fetch(meta, (oth0, oth1), 3 * out_rows, out_rows, wo_oth, sems_oth)
    in_first_step(copies, "start")
    wide = w_ff.shape[-1]
    ff = dup_out.shape[-1]
    parts = ff // wide
    tall = w_ff.shape[2] // (2 * parts)

    @pl.when(pl.program_id(0) == 0)
    def _():
        sums_u[...] = jnp.zeros_like(sums_u)
        sums_d[...] = jnp.zeros_like(sums_d)

    low_in = dblock_low[...]
    dnorm = None
    for n in range(2 * parts):
        side, c = divmod(n, parts)
        at_side = meta[TP] if side == 0 else 1 - meta[TP]
        at = slice(c * wide, (c + 1) * wide)
        down = slice((parts + c) * tall, (parts + c + 1) * tall)
        dact = dot_nn(low_in, flat(w_ff[:, at_side, down, :]))
        dpre = dact * slope[:, side * ff + c * wide : side * ff + (c + 1) * wide].astype(F32)
        dup = dpre.astype(LOW)
        if side == 0:
            dup_out[:, at] = dup
            sums_u[0:1, at] += colsum(dpre)
        part = dot_nt(dup, flat(w_ff[:, at_side, c * tall : (c + 1) * tall, :]))
        dnorm = part if dnorm is None else dnorm + part
    normed = normed_in[...].astype(F32)
    sums_d[0:1, :] += colsum(dnorm * normed)
    sums_d[1:2, :] += colsum(dnorm)
    dresid = dblock[...] + norm_back(dnorm * vecs[3:4], normed, inv_in[:, 0:1])
    sums_d[2:3, :] += colsum(dresid)
    dresid_out[...] = dresid
    low = dresid.astype(LOW)
    dresid_low_out[...] = low
    in_first_step(copies, "wait")
    dmixed_own_out[...] = dot_nn(low, flat(wo_own[...])).astype(LOW)
    dmixed_oth_out[...] = dot_nn(low, flat(wo_oth[...])).astype(LOW)


def tok_bwd_kernel(
    meta, tok, dproj_own, dproj_oth, dresid, own0, own1, oth0, oth1, vecs, g_tok, sums,
    w_own, w_oth, sems_own, sems_oth,
):
    copies = fetch(meta, (own0, own1), 0, w_own.shape[2], w_own, sems_own)
    copies += fetch(meta, (oth0, oth1), 0, w_oth.shape[2], w_oth, sems_oth)
    in_first_step(copies, "start")
    normed, inv = norm_parts(tok[...].astype(F32))

    @pl.when(pl.program_id(0) == 0)
    def _():
        sums[...] = jnp.zeros_like(sums)

    in_first_step(copies, "wait")
    dnorm = None
    for dproj, w in ((dproj_own, w_own), (dproj_oth, w_oth)):
        rows = w.shape[2] // 3
        for t in range(3):
            part = dot_nt(dproj[t], flat(w[:, :, t * rows : (t + 1) * rows, :]))
            dnorm = part if dnorm is None else dnorm + part
    sums[0:1, :] += colsum(dnorm * normed)
    sums[1:2, :] += colsum(dnorm)
    g_tok[...] = dresid[...] + norm_back(dnorm * vecs[0:1], normed, inv)


def weight_grads(meta, products, apart):
    arrays, where = [], {}
    for left, right, _ in products:
        for arr in (left, right):
            if id(arr) not in where:
                where[id(arr)] = len(arrays)
                arrays.append(arr)
    plan, at = [], 0
    for left, right, index in products:
        rows = left.shape[1] // SHARDS
        plan.append((where[id(left)], where[id(right)], index, at, rows))
        at += rows
    total, cols = at, products[0][1].shape[-1]
    n_in, n_out = len(arrays), 2 if apart else 1

    def kernel(meta, *refs):
        ins, outs = refs[:n_in], refs[n_in : n_in + n_out]
        held, (stage, sems_in, sems_out) = refs[n_in + n_out : -3], refs[-3:]
        core = meta[CORE]
        loads = [
            pltpu.make_async_copy(ref, buf, sems_in.at[i]) for i, (ref, buf) in enumerate(zip(ins, held))
        ]
        for load in loads:
            load.start()
        waited, stores = set(), []
        for n, (left, right, index, at, rows) in enumerate(plan):
            for i in (left, right):
                if i not in waited:
                    waited.add(i)
                    loads[i].wait()
            other = held[right][...] if index is None else held[right][index]
            grad = dot_tn(held[left][...], other).astype(LOW)
            stage[:, :, at : at + rows, :] = grad.reshape(SHARDS // 2, 2, rows, cols)
            for i, out in enumerate(outs):
                frm, to = stage.at[:, :, at : at + rows, :], out.at[..., at : at + rows, :]
                if apart:
                    frm = stage.at[:, core if i == 0 else 1 - core, at : at + rows, :]
                store = pltpu.make_async_copy(frm, to, sems_out.at[n_out * n + i])
                store.start()
                stores.append(store)
        for store in stores:
            store.wait()

    shape = sds((SHARDS // 2, *(() if apart else (2,)), total, cols), LOW)
    macs = sum(left.shape[0] * left.shape[1] * cols for left, _, _ in products)
    return run(
        kernel, meta, 1,
        [(arr, ANY) for arr in arrays],
        [(shape, ANY)] * n_out,
        scratch=[pltpu.VMEM(arr.shape, LOW) for arr in arrays]
        + [
            pltpu.VMEM((SHARDS // 2, 2, total, cols), LOW),
            pltpu.SemaphoreType.DMA((n_in,)),
            pltpu.SemaphoreType.DMA((n_out * len(plan),)),
        ],
        flops=2 * macs,
        nbytes=4 * SHARDS * total * cols,
    )


SWAP = [(0, 1), (1, 0)]
SWAP_CORE = [(i, i ^ 1) for i in range(SHARDS)]
SWAP_Y = [(i, i ^ 2) for i in range(SHARDS)]
hold = lax.optimization_barrier


def shift_z(step):
    return [(z * 4 + r, ((z + step) % 4) * 4 + r) for z in range(4) for r in range(4)]


def place(n_dp):
    if n_dp != SHARDS:
        zero = jnp.zeros((), jnp.int32)
        return zero, zero, zero
    at = lax.axis_index("dp")
    return at // 4, (at // 2) % 2, at % 2


def pick(arr, i, axis):
    return lax.dynamic_index_in_dim(arr, i, axis, keepdims=False)


def regroup(full):
    n_dp = full.shape[0]
    per = n_dp // SHARDS
    mid = full.shape[1:-2]
    split = full.reshape(SHARDS, per, *mid, *full.shape[-2:])
    order = (0, *range(2, 2 + len(mid)), 1, 2 + len(mid), 3 + len(mid))
    return jnp.transpose(split, order).reshape(SHARDS, *mid, per * full.shape[-2], full.shape[-1])


def by_core(full):
    _, n, rows, cols = full.shape
    split = full.reshape(SHARDS // 2, 2, n * rows, cols)
    return split[:, 0], split[:, 1]


def gather_both(group, n_dp):
    full = lax.all_gather(group, ("dp", "tp"), axis=0).reshape(n_dp, 2, *group.shape)
    full = regroup(full)
    tp = lax.axis_index("tp")
    return pick(full, tp, 1), pick(full, 1 - tp, 1)


class Gather:
    def __init__(self, block, where):
        self.block, (self.z, self.y, _) = block, where
        self.from_y = lax.ppermute(block, "dp", SWAP_Y)
        self.along_z = [lax.ppermute(block, "dp", shift_z(s)) for s in (1, 2, 3)]

    def cross_y(self):
        self.rest = lax.ppermute(jnp.stack(self.along_z), "dp", SWAP_Y)

    def finish(self):
        buf = jnp.zeros((4, 2, *self.block.shape), LOW)
        zero = jnp.zeros((), jnp.int32)
        for s in range(4):
            at = (self.z - s) % 4
            mine = self.block if s == 0 else self.along_z[s - 1]
            theirs = self.from_y if s == 0 else self.rest[s - 1]
            for piece, y in ((mine, self.y), (theirs, 1 - self.y)):
                buf = lax.dynamic_update_slice(buf, piece[None, None], (at, y, zero, zero))
        return buf.reshape(8, *self.block.shape)


def swap_core(block):
    return lax.ppermute(block, "dp", SWAP_CORE)


def gather_ff(w_up, w_down, wide, n_dp):
    cols = lambda w: jnp.transpose(w.reshape(w.shape[0], -1, wide), (1, 0, 2))
    parts = jnp.concatenate([cols(w_up), cols(w_down)])
    full = lax.all_gather(parts, ("dp", "tp"), axis=0).reshape(n_dp, 2, *parts.shape)
    return regroup(full).reshape(SHARDS, 2, -1, wide)


def pack_head(w_hid1, w_hid2, w_mod):
    t, rows, cols = w_mod.shape
    wide = w_hid1.shape[1]
    mod = jnp.transpose(w_mod.reshape(t, rows, cols // wide, wide), (0, 2, 1, 3))
    return jnp.stack([w_hid1, w_hid2]), mod.reshape(-1, rows, wide)


class Scatter:
    def __init__(self, here, there, where):
        self.z, self.y, _ = where
        part = (here.astype(F32) + swap_core(there).astype(F32)).astype(LOW)
        self.part = part.reshape(4, 2, *here.shape[1:])

    def start_y(self):
        self.got = lax.ppermute(pick(self.part, 1 - self.y, 1), "dp", SWAP_Y)

    def add_y(self):
        self.part = (pick(self.part, self.y, 1).astype(F32) + self.got.astype(F32)).astype(LOW)

    def start_z(self):
        self.got = [
            lax.ppermute(pick(self.part, (self.z + s) % 4, 0), "dp", shift_z(s)) for s in (1, 2, 3)
        ]

    def result(self):
        total = pick(self.part, self.z, 0).astype(F32)
        for got in self.got:
            total = total + got.astype(F32)
        return total


class ScatterAny:
    def __init__(self, here, there, rows, n_dp):
        self.total = scatter_whole(jnp.stack([here, there], axis=1), rows, n_dp)
        self.part = self.got = jnp.zeros((), LOW)

    def start_y(self):
        pass

    add_y = start_z = start_y

    def result(self):
        return self.total


def scatter_whole(packed, rows, n_dp):
    packed = packed.reshape(SHARDS, *packed.shape[2:])
    per = n_dp // SHARDS
    if per > 1:
        parts, at = [], 0
        for r in rows:
            part = packed[:, at : at + r]
            parts.append(part.reshape(n_dp, r // per, packed.shape[-1]))
            at += r
        packed = jnp.concatenate(parts, axis=1)
    return lax.psum_scatter(packed, "dp", scatter_dimension=0, tiled=False).astype(F32)


def sum_all(vector, n_dp):
    if n_dp != SHARDS:
        return lax.psum(vector, "dp")
    for swap in (SWAP_CORE, SWAP_Y, [(i, i ^ 4) for i in range(16)], [(i, i ^ 8) for i in range(16)]):
        vector = vector + lax.ppermute(vector, "dp", swap)
    return vector


def on_device(
    tokens, latents, grad_block, grad_head, image_lengths, ln1_gain, ln1_bias, w_qkv, b_qv, w_out,
    b_out, ln2_gain, ln2_bias, w_up, b_up, w_down, b_down, w_mod, b_mod, w_hid1, b_hid1, w_hid2,
    b_hid2,
):
    rows, width = tokens.shape
    head_width = latents.shape[1]
    half = w_qkv.shape[2]
    ff = w_up.shape[1]
    hid = w_hid1.shape[1]
    n_dp = width // w_out.shape[0]
    direct = n_dp == SHARDS
    tp = lax.axis_index("tp")
    where = place(n_dp)
    core = where[2]
    pairs = half // 128
    tall, short = rows // 2, rows // 4
    out_rows, in_rows = width // SHARDS, head_width // SHARDS

    early = jnp.concatenate([w_qkv.reshape(-1, half), w_out])
    hid_part, mod_part = pack_head(w_hid1, w_hid2, w_mod)
    if direct:
        gather_one = Gather(early, where)
        gather_one.cross_y()
        own_first = gather_one.finish()
        early_own = (own_first, swap_core(own_first))
        across = lax.ppermute(own_first, "tp", SWAP)
        late = jnp.concatenate([hid_part.reshape(-1, hid), mod_part.reshape(-1, hid)])
        late, _ = hold((late, gather_one.along_z))
        gather_two = Gather(late, where)
    else:
        got = gather_both(jnp.concatenate([w_qkv, w_out[None]]), n_dp)
        early_own, early_oth = by_core(got[0]), by_core(got[1])
        hid_own, hid_oth = gather_both(hid_part, n_dp)
        mod_all = regroup(lax.all_gather(mod_part, "dp", axis=0))
        late_own = tuple(
            jnp.concatenate([h, m], axis=1) for h, m in zip(by_core(hid_own), by_core(mod_all))
        )
        late_oth = by_core(hid_oth)
    w_ff = gather_ff(w_up, w_down, hid, n_dp)

    mine = jnp.concatenate([b_qv.reshape(-1), b_up, b_hid1])
    theirs = lax.ppermute(mine, "tp", SWAP)
    cut = lambda v: (v[: 2 * half].reshape(2, half), v[2 * half : 2 * half + ff], v[2 * half + ff :])
    (bqv_own, bup_own, bhid_own), (bqv_oth, bup_oth, bhid_oth) = cut(mine), cut(theirs)
    b_up2 = jnp.stack([bup_own, bup_oth])
    b_hid2x = jnp.stack([bhid_own, bhid_oth])
    vecs = jnp.stack([ln1_gain, ln1_bias, b_out, ln2_gain, ln2_bias, b_down])
    last_bias = b_hid2.reshape(1, -1)

    ends = jnp.cumsum(image_lengths[0])
    meta = jnp.concatenate([tp.reshape(1), core.reshape(1), ends]).astype(jnp.int32)
    at = jnp.arange(rows, dtype=jnp.int32)[:, None]
    segment = jnp.sum((at >= ends[None, :]).astype(jnp.int32), axis=1, keepdims=True)
    lane_of = (jnp.arange(128) % HDIM)[None, :]
    same = segment == lane_of
    seg_q = jnp.where(same & (lane_of < 4), 1.0, 0.0).astype(LOW)
    seg_k = jnp.where(jnp.logical_not(same) & (lane_of < 4), FAR, 0.0).astype(LOW)

    tall3 = pl.BlockSpec((3, tall, half), lambda i, meta: (0, i, 0))
    keep = lambda n, w: (sds((n, w), F32), sum_spec(n, w))
    pair_spec = pl.BlockSpec((rows, 128), lambda p, meta: (0, p))
    whole = pl.BlockSpec((rows, 128), lambda p, meta: (0, 0))
    part_spec = lambda t: pl.BlockSpec((None, rows, 128), lambda p, meta: (t, 0, p))
    proj_shape = (sds((3, rows, half), LOW), tall3)
    attn_cost = rows * rows * 256 * 2 * pairs
    vec_in = (vecs, const_spec(*vecs.shape))
    pair_in = lambda pair: [(pair[0], ANY), (pair[1], ANY)]
    pair_buf = lambda n, cols: pltpu.VMEM((SHARDS // 2, 2, n, cols), LOW)
    two_sems = pltpu.SemaphoreType.DMA((2,))

    def attend(proj):
        return run(
            attn_fwd_kernel, meta, pairs,
            [
                (proj, part_spec(0)), (proj, part_spec(1)), (proj, part_spec(2)),
                (seg_q, whole), (seg_k, whole),
            ],
            [(sds((rows, half), LOW), pair_spec), (sds((rows, half), F32), pair_spec)],
            flops=4 * attn_cost,
            nbytes=12 * rows * half,
            exps=2 * pairs * rows * rows,
        )

    def attend_back(proj, dmixed, mixed, total):
        return run(
            attn_bwd_kernel, meta, pairs,
            [
                (proj, part_spec(0)), (proj, part_spec(1)), (proj, part_spec(2)),
                (dmixed, pair_spec), (mixed, pair_spec), (total, pair_spec),
                (seg_q, whole), (seg_k, whole),
            ],
            [
                (sds((3, rows, half), LOW), pl.BlockSpec((3, rows, 128), lambda p, meta: (0, 0, p))),
                (sds((8, half), F32), pl.BlockSpec((8, 128), lambda p, meta: (0, p))),
            ],
            flops=10 * attn_cost,
            nbytes=20 * rows * half,
            exps=2 * pairs * rows * rows,
        )

    norm_one, proj_own = run(
        qkv_own_kernel, meta, 2,
        [
            (tokens, row_spec(tall, width)), vec_in, *pair_in(early_own),
            (bqv_own, const_spec(2, half)),
        ],
        [(sds((rows, width), LOW), row_spec(tall, width)), proj_shape],
        scratch=[pair_buf(3 * out_rows, half), two_sems],
        flops=6 * rows * width * half,
        nbytes=10 * rows * width,
    )
    if direct:
        across, proj_own = hold((across, proj_own))
    mixed_own, total_own = attend(proj_own)
    if direct:
        early_oth = (across, swap_core(across))
        gather_two.along_z, mixed_own = hold((gather_two.along_z, mixed_own))
        gather_two.cross_y()
    (proj_oth,) = run(
        qkv_other_kernel, meta, 2,
        [
            (norm_one, row_spec(tall, width)), *pair_in(early_oth),
            (bqv_oth, const_spec(2, half)),
        ],
        [proj_shape],
        scratch=[pair_buf(3 * out_rows, half), two_sems],
        flops=6 * rows * width * half,
        nbytes=8 * rows * width,
    )
    mixed_oth, total_oth = attend(proj_oth)
    if direct:
        gather_two.rest, mixed_oth = hold((gather_two.rest, mixed_oth))
        late_first = gather_two.finish()
        late_own = (late_first, swap_core(late_first))
        late_across = lax.ppermute(late_first[:, : 2 * in_rows], "tp", SWAP)

    early_in = pair_in(early_own) + pair_in(early_oth)
    ff_block = const_spec(*w_ff.shape)
    norm_two, normed_two, inv_two, act, slope, block, block_low, stats = run(
        ff_fwd_kernel, meta, 4,
        [
            (tokens, row_spec(short, width)), (mixed_own, row_spec(short, half)),
            (mixed_oth, row_spec(short, half)), *early_in, (w_ff, ff_block), vec_in,
            (b_up2, const_spec(2, ff)),
        ],
        [
            (sds((rows, width), LOW), row_spec(short, width)),
            (sds((rows, width), LOW), row_spec(short, width)),
            (sds((rows, 128), F32), row_spec(short, 128)),
            (sds((rows, ff), LOW), row_spec(short, ff)),
            (sds((rows, 2 * ff), LOW), row_spec(short, 2 * ff)),
            (sds((rows, width), F32), row_spec(short, width)),
            (sds((rows, width), LOW), row_spec(short, width)),
            keep(8, width),
        ],
        scratch=[pair_buf(out_rows, half), pair_buf(out_rows, half), two_sems, two_sems],
        flops=2 * rows * width * (4 * ff + width),
        nbytes=rows * (20 * width + 6 * ff) + 8 * width * ff,
        exps=4 * rows * ff,
    )
    if direct:
        late_across, block = hold((late_across, block))
        late_oth = (late_across, swap_core(late_across))

    (
        head_out, grad_latents, hid_in, hidden, branch_low, pre_low, mod_low, cond, dblock,
        dblock_low, sums_w, sums_h, sums_b,
    ) = run(
        head_kernel, meta, 4,
        [
            (block, row_spec(short, width)), (latents, row_spec(short, head_width)),
            (grad_block, row_spec(short, width)), (grad_head, row_spec(short, head_width)),
            *pair_in(late_own), *pair_in(late_oth),
            (b_mod, const_spec(3, head_width)), (b_hid2x, const_spec(2, hid)),
            (last_bias, const_spec(1, head_width)),
        ],
        [
            (sds((rows, head_width), LOW), row_spec(short, head_width)),
            (sds((rows, head_width), F32), row_spec(short, head_width)),
            (sds((rows, head_width), LOW), row_spec(short, head_width)),
            (sds((rows, hid), LOW), row_spec(short, hid)),
            (sds((rows, head_width), LOW), row_spec(short, head_width)),
            (sds((rows, hid), LOW), row_spec(short, hid)),
            (sds((3, rows, hid), LOW), pl.BlockSpec((3, short, hid), lambda i, meta: (0, i, 0))),
            (sds((rows, width), LOW), row_spec(short, width)),
            (sds((rows, width), F32), row_spec(short, width)),
            (sds((rows, width), LOW), row_spec(short, width)),
            keep(8, head_width), keep(8, hid), keep(8, width),
        ],
        scratch=[
            pair_buf(late_own[0].shape[1], hid), pair_buf(2 * in_rows, hid), two_sems, two_sems,
        ],
        flops=2 * rows * head_width * (6 * width + 4 * head_width),
        nbytes=rows * (14 * width + 22 * head_width) + 20 * head_width * head_width,
        exps=rows * 2 * head_width,
    )

    def scatter(products):
        here, there = weight_grads(meta, products, True)
        if direct:
            return Scatter(here, there, where)
        return ScatterAny(here, there, [p[0].shape[1] // SHARDS for p in products], n_dp)

    products = [
        (hid_in, pre_low, None), (branch_low, hidden, None), (cond, mod_low, 0),
        (cond, mod_low, 1), (cond, mod_low, 2),
    ]
    (packed,) = weight_grads(meta, products, False)
    packed, dblock_low = hold((packed, dblock_low))
    got_head = scatter_whole(packed, [p[0].shape[1] // SHARDS for p in products], n_dp)
    down = scatter([(dblock_low, act, None)])
    down.part, dblock = hold((down.part, dblock))
    down.start_y()

    dup, dresid, dresid_low, dmixed_own, dmixed_oth, sums_u, sums_r = run(
        ff_bwd_kernel, meta, 2,
        [
            (dblock, row_spec(tall, width)), (dblock_low, row_spec(tall, width)),
            (slope, row_spec(tall, 2 * ff)), (normed_two, row_spec(tall, width)),
            (inv_two, row_spec(tall, 128)), *early_in, (w_ff, ff_block), vec_in,
        ],
        [
            (sds((rows, ff), LOW), row_spec(tall, ff)),
            (sds((rows, width), F32), row_spec(tall, width)),
            (sds((rows, width), LOW), row_spec(tall, width)),
            (sds((rows, half), LOW), row_spec(tall, half)),
            (sds((rows, half), LOW), row_spec(tall, half)),
            keep(8, ff), keep(8, width),
        ],
        scratch=[pair_buf(out_rows, half), pair_buf(out_rows, half), two_sems, two_sems],
        flops=2 * rows * width * (4 * ff + width),
        nbytes=rows * (16 * width + 6 * ff) + 8 * width * ff,
    )
    up = scatter([(norm_two, dup, None)])
    down.got, up.part, dmixed_own = hold((down.got, up.part, dmixed_own))
    down.add_y()
    down.part, up.part, dmixed_own = hold((down.part, up.part, dmixed_own))
    down.start_z()
    up.start_y()

    dproj_own, sums_qv = attend_back(proj_own, dmixed_own, mixed_own, total_own)
    down.got, up.got, dproj_own = hold((down.got, up.got, dproj_own))
    up.add_y()
    up.part, dproj_own = hold((up.part, dproj_own))
    up.start_z()
    attn = scatter(
        [(norm_one, dproj_own, 0), (norm_one, dproj_own, 1), (norm_one, dproj_own, 2), (dresid_low, mixed_own, None)]
    )
    attn.part, dmixed_oth = hold((attn.part, dmixed_oth))
    attn.start_y()
    dproj_oth, _ = attend_back(proj_oth, dmixed_oth, mixed_oth, total_oth)
    up.got, attn.got, got_head, dproj_oth = hold((up.got, attn.got, got_head, dproj_oth))
    attn.add_y()
    attn.part, dproj_oth = hold((attn.part, dproj_oth))
    attn.start_z()
    w_rows, w_in = width // n_dp, head_width // n_dp
    mod_mine = got_head[2 * w_in :].reshape(3, -1, hid)
    mod_theirs = lax.ppermute(mod_mine, "tp", SWAP)
    grad_tokens, sums_t = run(
        tok_bwd_kernel, meta, 2,
        [
            (tokens, row_spec(tall, width)), (dproj_own, tall3), (dproj_oth, tall3),
            (dresid, row_spec(tall, width)), *early_in, vec_in,
        ],
        [(sds((rows, width), F32), row_spec(tall, width)), keep(8, width)],
        scratch=[pair_buf(3 * out_rows, half), pair_buf(3 * out_rows, half), two_sems, two_sems],
        flops=2 * rows * width * 3 * width,
        nbytes=16 * rows * width,
    )

    pieces = [
        sums_t[0:2].reshape(-1), sums_qv[0:2].reshape(-1), sums_r[0:3].reshape(-1),
        sums_u[0], sums_b[0], sums_w[0:4].reshape(-1), sums_h[0],
    ]
    sizes = [p.shape[0] for p in pieces]
    joined = jnp.concatenate(pieces)
    joined = jnp.pad(joined, (0, -joined.shape[0] % 1024)).reshape(-1, 128)
    summed = sum_all(joined, n_dp).reshape(-1)
    split, begin = [], 0
    for size in sizes:
        split.append(summed[begin : begin + size])
        begin += size
    ln1s, bqv, rs, d_b_up, d_b_down, ws, d_b_hid1 = split
    ln1s, bqv, rs = ln1s.reshape(2, -1), bqv.reshape(2, -1), rs.reshape(3, -1)
    ws = ws.reshape(4, -1)

    d_w_hid1, d_w_hid2 = got_head[:w_in], got_head[w_in : 2 * w_in]
    first = tp == 0
    d_w_mod = jnp.concatenate(
        [jnp.where(first, mod_mine, mod_theirs), jnp.where(first, mod_theirs, mod_mine)], axis=2
    )
    got = attn.result()
    d_w_qkv = got[: 3 * w_rows].reshape(3, w_rows, half)
    d_w_out = got[3 * w_rows :]

    squares = jnp.concatenate([jnp.sum(stats[0:3], axis=1), jnp.sum(sums_w[4:5], axis=1)])
    widths = jnp.array([width, width, width, head_width], F32)
    count = jnp.clip(ends[2], 0, rows).astype(F32)
    rms_values = jnp.sqrt(squares / (count * widths)).reshape(1, 4)
    return (
        block_low, head_out, grad_tokens, grad_latents, ln1s[0], ln1s[1], d_w_qkv, bqv, d_w_out,
        rs[2], rs[0], rs[1], up.result(), d_b_up, down.result(), d_b_down, d_w_mod, ws[1:4], d_w_hid1,
        d_b_hid1, d_w_hid2, ws[0], rms_values,
    )


def solution(mesh):
    rows, one = P("dp", None), P()
    split = P("dp", "tp")
    weights = (
        one, one, P(None, "dp", "tp"), P(None, "tp"), split, one, one, one, split, P("tp"), split,
        one, P(None, "dp", None), one, split, P("tp"), split, one,
    )
    return jax.shard_map(
        on_device,
        mesh=mesh,
        in_specs=(rows, rows, rows, rows, rows) + weights,
        out_specs=(rows, rows, rows, rows) + weights + (rows,),
        check_vma=False,
    )
```

time: 646 us -> 430 us (0.67)
  waiting for transfers between devices: 299 us -> 59.5 us
  starting transfers between devices: 4.78 us -> 65 us
  matrix products: 24.3 us -> 0 us
  blocking collectives: 22.4 us -> 0 us
  Pallas kernels: 215 us -> 231 us
    all_gather x4 -> x1, waiting for transfers between devices: 167 us -> 0.01 us  [gather_ff(): lax.all_gather(parts, ('dp', 'tp'), axis=0).reshape(n_dp, 2, *parts.shape)]
    reduce_scatter x3 -> x1, waiting for transfers between devices: 129 us -> 0.02 us  [scatter_whole(): lax.psum_scatter(packed, 'dp', scatter_dimension=0, tiled=False).astype(F32)]
    ppermute x2 -> x37, starting transfers between devices: 4.5 us -> 65 us  [the longest x9 30.4 us: start_z(): lax.ppermute(pick(self.part, (self.z + s) % 4, 0), 'dp', shift_z(s))]
    ppermute x2 -> x37, waiting for transfers between devices: 2.25 us -> 59.4 us  [the longest x2 17.1 us: cross_y(): self.rest = lax.ppermute(jnp.stack(self.along_z), 'dp', SWAP_Y)]
    dot_general x7 -> x0, matrix products: 24.3 us -> none  [the longest x5 13.4 us: dot_tn(): lax.dot_general(a, b, (((0,), (0,)), ((), ())), preferred_element_type=F32)]
    all_gather x1 -> x0, blocking collectives: 22.4 us -> none  [on_device(): summed = jnp.sum(lax.all_gather(joined, 'dp', axis=0), axis=0).reshape(-1)]
    pallas_call x7 -> x14, Pallas kernels: 215 us -> 231 us  [run(): pl.pallas_call(kernel, grid_spec=pltpu.PrefetchScalarGridSpec(num_scalar_...]
    dynamic_update_slice x0 -> x15, local copies, waits for them, and re-layouts: none -> 12.1 us  [finish(): buf = lax.dynamic_update_slice(buf, piece[None, None], (at, y, zero, zero))]
  transfers between devices with their start and end apart: 9 -> 39, of which waited for: 7 -> 12; matrix products, arithmetic and copies ran while one was open for 10% -> 11% of each run, Pallas kernels for 15% -> 30%
where the time goes in v2:
time: 430 us; the launch traced here: 426 us
  Pallas kernels  231 us (54%)
  starting transfers between devices  65 us (15%)
  waiting for transfers between devices  59.5 us (14%)
  local copies, waits for them, and re-layouts  34.1 us (8%)
  other arithmetic  20.7 us (5%)
  between operations  16 us (4%)
    pallas_call x14, Pallas kernels, run(): pl.pallas_call(kernel, grid_spec=pltpu.PrefetchScalarGridSpec(num_scalar_...  231 us
    ppermute x9, starting transfers between devices, start_z(): lax.ppermute(pick(self.part, (self.z + s) % 4, 0), 'dp', shift_z(s))  30.4 us
    ppermute x6, starting transfers between devices, __init__(): self.along_z = [lax.ppermute(block, 'dp', shift_z(s)) for s in (1, 2, 3)]  18.6 us
    ppermute x2, waiting for transfers between devices, cross_y(): self.rest = lax.ppermute(jnp.stack(self.along_z), 'dp', SWAP_Y)  17.1 us
    ppermute x3, waiting for transfers between devices, start_y(): self.got = lax.ppermute(pick(self.part, 1 - self.y, 1), 'dp', SWAP_Y)  12.2 us
    dynamic_update_slice x15, local copies, waits for them, and re-layouts, finish(): buf = lax.dynamic_update_slice(buf, piece[None, None], (at, y, zero, zero))  12.1 us
  transfers between devices with their start and end apart: 39, of which 12 were waited for; matrix products, arithmetic and copies ran while one was open for 11% of the time, Pallas kernels for 30%

profile of v2, /device:TPU:0, one launch (start us, length us, event | category | flops | bytes accessed | tf_op | source)
XLA Modules:
  0.0 425.9 jit_solution(5144290804765654637)
XLA Ops:
  10.5 3.1 collective-permute-start
  13.5 2.6 collective-permute-start.1
  22.8 3.0 collective-permute-done.1
  28.9 9.1 %collective-permute-done.7 = bf16[3,192,384]{2,1,0:T(8,128)(2,1)S(1)} collective-permute-done((bf16[3,192,384]{2,1,0:T(8,128)(2,1)S(1)}, bf16[3,192,384]{2,1,0:T(8,128)(2,1)S(1)}, u32[]{:S(2)}, u32[]{:S(2)}) %collective-permute-start.7) | collective-permute-done | bytes 442400 | tf_op jit(solution)/shard_map/ppermute | solution.py:583
  48.5 9.0 %collective-permute-start.3 = (bf16[416,512]{1,0:T(8,128)(2,1)}, bf16[416,512]{1,0:T(8,128)(2,1)}, u32[]{:S(2)}, u32[]{:S(2)}) collective-permute-start(bf16[416,512]{1,0:T(8,128)(2,1)} %pad_maximum_fusion.3), channel_id=1, source_target_pairs={{0,8},{2,10},{4,12},{6,14},{8,16},{10,18},{12,20},{14,22},{16,24},... | collective-permute-start | bytes 1277960 | tf_op jit(solution)/shard_map/ppermute | solution.py:580
  58.8 2.6 collective-permute-start.5
  61.4 8.1 %shard_map.407 = (bf16[1088,768]{1,0:T(8,128)(2,1)}, bf16[3,1088,384]{2,1,0:T(8,128)(2,1)}) custom-call(s32[5]{0:T(128)} %pad_add_fusion.meta, bf16[1088,768]{1,0:T(8,128)(2,1)} %tok.5, f32[6,768]{1,0:T(8,128)} %stack.85.vecs, bf16[8,192,384]{2,1,0:T(8,128)(2,1)} %bitcast.21.w0.own0, bf16[8,192,384]{2,1,0:T(8,128)(2,1)} %collective-permute-done.9.w1.own1, ...), custom_call_target="tpu_custom_call" | custom-call | flops 1925185536 | bytes 8355840 | tf_op jit(solution)/shard_map/pallas_call | solution.py:104
  69.5 8.3 %collective-permute-done.8.w0.oth0 = bf16[8,192,384]{2,1,0:T(8,128)(2,1)} collective-permute-done((bf16[8,192,384]{2,1,0:T(8,128)(2,1)}, bf16[8,192,384]{2,1,0:T(8,128)(2,1)}, u32[]{:S(2)}, u32[]{:S(2)}) %collective-permute-start.8) | collective-permute-done | bytes 1179680 | tf_op jit(solution)/shard_map/ppermute | solution.py:700
  77.8 14.5 %shard_map.408 = (bf16[1088,384]{1,0:T(8,128)(2,1)}, f32[1088,384]{1,0:T(8,128)}) custom-call(s32[5]{0:T(128)} %pad_add_fusion.meta, bf16[3,1088,384]{2,1,0:T(8,128)(2,1)} %get-tuple-element.108.q.k.v, bf16[3,1088,384]{2,1,0:T(8,128)(2,1)} %get-tuple-element.108.q.k.v, bf16[3,1088,384]{2,1,0:T(8,128)(2,1)} %get-tuple-element.108.q.k.v, ...), custom_call_target="tpu_custom_call" | custom-call | flops 7272923136 | bytes 5013504 | tf_op jit(solution)/shard_map/pallas_call | solution.py:104
  92.3 4.0 collective-permute-done.5
  96.3 2.3 pad_maximum_fusion
  100.8 7.4 %shard_map.409.q.k.v = bf16[3,1088,384]{2,1,0:T(8,128)(2,1)} custom-call(s32[5]{0:T(128)} %pad_add_fusion.meta, bf16[1088,768]{1,0:T(8,128)(2,1)} %get-tuple-element.114.norm_one.refs_0_, bf16[8,192,384]{2,1,0:T(8,128)(2,1)} %collective-permute-done.8.w0.oth0, bf16[8,192,384]{2,1,0:T(8,128)(2,1)} %collective-permute-done.11.w1.oth1, f32[2,384]{1,0:T(2,128)} %reshape.203.b_qv), custom_call_target="tpu_custom_call" | custom-call | flops 1925185536 | bytes 6684672 | tf_op jit(solution)/shard_map/pallas_call | solution.py:104
  108.2 14.4 %shard_map.410 = (bf16[1088,384]{1,0:T(8,128)(2,1)}, f32[1088,384]{1,0:T(8,128)}) custom-call(s32[5]{0:T(128)} %pad_add_fusion.meta, bf16[3,1088,384]{2,1,0:T(8,128)(2,1)} %shard_map.409.q.k.v, bf16[3,1088,384]{2,1,0:T(8,128)(2,1)} %shard_map.409.q.k.v, bf16[3,1088,384]{2,1,0:T(8,128)(2,1)} %shard_map.409.q.k.v, bf16[1088,128]{1,0:T(8,128)(2,1)} %get-tuple-element.210.seg_q, ...), custom_call_target="tpu_custom_call" | custom-call | flops 7272923136 | bytes 5013504 | tf_op jit(solution)/shard_map/pallas_call | solution.py:104
  122.6 8.0 %collective-permute-done.10 = bf16[3,416,512]{2,1,0:T(8,128)(2,1)} collective-permute-done((bf16[3,416,512]{2,1,0:T(8,128)(2,1)}, bf16[3,416,512]{2,1,0:T(8,128)(2,1)}, u32[]{:S(2)}, u32[]{:S(2)}) %collective-permute-start.10) | collective-permute-done | bytes 1277984 | tf_op jit(solution)/shard_map/ppermute | solution.py:583
  138.4 29.5 %shard_map.411 = (bf16[1088,768]{1,0:T(8,128)(2,1)}, bf16[1088,768]{1,0:T(8,128)(2,1)}, f32[1088,128]{1,0:T(8,128)}, bf16[1088,1536]{1,0:T(8,128)(2,1)}, bf16[10...) custom-call(s32[5]{0:T(128)} %pad_add_fusion.meta, ...), custom_call_target="tpu_custom_call" | custom-call | flops 11551113216 | bytes 36175872 | tf_op jit(solution)/shard_map/pallas_call | solution.py:104
  168.6 2.4 collective-permute-done.16.oth1
  171.0 38.4 %shard_map.412 = (bf16[1088,1024]{1,0:T(8,128)(2,1)}, f32[1088,1024]{1,0:T(8,128)}, bf16[1088,1024]{1,0:T(8,128)(2,1)}, bf16[1088,512]{1,0:T(8,128)(2,1)}, bf16[...) custom-call(s32[5]{0:T(128)} %pad_add_fusion.meta, ...), custom_call_target="tpu_custom_call" | custom-call | flops 19394461696 | bytes 57180160 | tf_op jit(solution)/shard_map/pallas_call | solution.py:104
  209.4 9.9 %shard_map.413 = bf16[8,2,272,512]{3,2,1,0:T(8,128)(2,1)} custom-call(s32[5]{0:T(128)} %pad_add_fusion.meta, bf16[1088,1024]{1,0:T(8,128)(2,1)} %get-tuple-element.124.refs_0_, bf16[1088,512]{1,0:T(8,128)(2,1)} %get-tuple-element.125.refs_1_, bf16[1088,1024]{1,0:T(8,128)(2,1)} %get-tuple-element.126.refs_2_, bf16[1088,512]{1,0:T(8,128)(2,1)} %get-tuple-element.127.refs_3_, ...), custom_call_target="tpu_custom_call" | custom-call | flops 4848615424 | bytes 8912896 | tf_op jit(solution)/shard_map/pallas_call | solution.py:104
  219.3 7.8 %shard_map.414 = (bf16[8,48,1536]{2,1,0:T(8,128)(2,1)}, bf16[8,48,1536]{2,1,0:T(8,128)(2,1)}) custom-call(s32[5]{0:T(128)} %pad_add_fusion.meta, bf16[1088,768]{1,0:T(8,128)(2,1)} %get-tuple-element.131.refs_0_.dblock_low, bf16[1088,1536]{1,0:T(8,128)(2,1)} %get-tuple-element.132.refs_1_), custom_call_target="tpu_custom_call" | custom-call | flops 2566914048 | bytes 4718592 | tf_op jit(solution)/shard_map/pallas_call | solution.py:104
  227.3 2.9 collective-permute-done.17
  231.8 23.2 %shard_map.415 = (bf16[1088,1536]{1,0:T(8,128)(2,1)}, f32[1088,768]{1,0:T(8,128)}, bf16[1088,768]{1,0:T(8,128)(2,1)}, bf16[1088,384]{1,0:T(8,128)(2,1)}, bf16[10...) custom-call(s32[5]{0:T(128)} %pad_add_fusion.meta, f32[1088,768]{1,0:T(8,128)} %get-tuple-element.138.dblock, ...), custom_call_target="tpu_custom_call" | custom-call | flops 11551113216 | bytes 32833536 | tf_op jit(solution)/shard_map/pallas_call | solution.py:104
  255.0 7.9 %shard_map.416 = (bf16[8,48,1536]{2,1,0:T(8,128)(2,1)}, bf16[8,48,1536]{2,1,0:T(8,128)(2,1)}) custom-call(s32[5]{0:T(128)} %pad_add_fusion.meta, bf16[1088,768]{1,0:T(8,128)(2,1)} %get-tuple-element.137.refs_0_, bf16[1088,1536]{1,0:T(8,128)(2,1)} %get-tuple-element.142.refs_1_), custom_call_target="tpu_custom_call" | custom-call | flops 2566914048 | bytes 4718592 | tf_op jit(solution)/shard_map/pallas_call | solution.py:104
  267.8 12.2 %collective-permute-done.18 = bf16[4,48,1536]{2,1,0:T(8,128)(2,1)} collective-permute-done((bf16[4,48,1536]{2,1,0:T(8,128)(2,1)}, bf16[4,48,1536]{2,1,0:T(8,128)(2,1)}, u32[]{:S(2)}, u32[]{:S(2)}) %collective-permute-start.18) | collective-permute-done | bytes 589856 | tf_op jit(solution)/shard_map/ppermute | solution.py:622
  281.8 19.2 %collective-permute-start.20 = (bf16[48,1536]{1,0:T(8,128)(2,1)S(1)}, bf16[48,1536]{1,0:T(8,128)(2,1)S(1)}, u32[]{:S(2)}, u32[]{:S(2)}) collective-permute-start(bf16[48,1536]{1,0:T(8,128)(2,1)S(1)} %get-tuple-element.199), channel_id=1, source_target_pairs={{0,8},{2,10},{4,12},{6,14},{8,16},{10,18},{12,20},{14,22},{16,24},... | collective-permute-start | bytes 442376 | tf_op jit(solution)/shard_map/ppermute | solution.py:629
  303.4 23.4 %shard_map.417 = (bf16[3,1088,384]{2,1,0:T(8,128)(2,1)}, f32[8,384]{1,0:T(8,128)}) custom-call(s32[5]{0:T(128)} %pad_add_fusion.meta, bf16[3,1088,384]{2,1,0:T(8,128)(2,1)} %get-tuple-element.108.q.k.v, bf16[3,1088,384]{2,1,0:T(8,128)(2,1)} %get-tuple-element.108.q.k.v, bf16[3,1088,384]{2,1,0:T(8,128)(2,1)} %get-tuple-element.108.q.k.v, ...), custom_call_target="tpu_custom_call" | custom-call | flops 18182307840 | bytes 8355840 | tf_op jit(solution)/shard_map/pallas_call | solution.py:104
  327.1 8.5 %shard_map.418 = (bf16[8,192,384]{2,1,0:T(8,128)(2,1)}, bf16[8,192,384]{2,1,0:T(8,128)(2,1)}) custom-call(s32[5]{0:T(128)} %pad_add_fusion.meta, bf16[1088,768]{1,0:T(8,128)(2,1)} %get-tuple-element.114.norm_one.refs_0_, bf16[3,1088,384]{2,1,0:T(8,128)(2,1)} %get-tuple-element.156.refs_1_.dproj_own, bf16[1088,768]{1,0:T(8,128)(2,1)} %get-tuple-element.157.refs_2_, ...), custom_call_target="tpu_custom_call" | custom-call | flops 2566914048 | bytes 4718592 | tf_op jit(solution)/shard_map/pallas_call | solution.py:104
  352.9 23.4 %shard_map.419 = (bf16[3,1088,384]{2,1,0:T(8,128)(2,1)}, f32[8,384]{1,0:T(8,128)}) custom-call(s32[5]{0:T(128)} %pad_add_fusion.meta, bf16[3,1088,384]{2,1,0:T(8,128)(2,1)} %shard_map.409.q.k.v, bf16[3,1088,384]{2,1,0:T(8,128)(2,1)} %shard_map.409.q.k.v, bf16[3,1088,384]{2,1,0:T(8,128)(2,1)} %shard_map.409.q.k.v, bf16[1088,384]{1,0:T(8,128)(2,1)} %get-tuple-element.164.g, ...), custom_call_target="tpu_custom_call" | custom-call | flops 18182307840 | bytes 8355840 | tf_op jit(solution)/shard_map/pallas_call | solution.py:104
  378.6 14.3 %shard_map.420 = (f32[1088,768]{1,0:T(8,128)}, f32[8,768]{1,0:T(8,128)}) custom-call(s32[5]{0:T(128)} %pad_add_fusion.meta, bf16[1088,768]{1,0:T(8,128)(2,1)} %tok.5, bf16[3,1088,384]{2,1,0:T(8,128)(2,1)} %get-tuple-element.156.refs_1_.dproj_own, bf16[3,1088,384]{2,1,0:T(8,128)(2,1)} %get-tuple-element.169.dproj_oth, f32[1088,768]{1,0:T(8,128)} %get-tuple-element.170.dresid, ...), custom_call_target="tpu_custom_call" | custom-call | flops 3850371072 | bytes 13369344 | tf_op jit(solution)/shard_map/pallas_call | solution.py:104
  396.4 2.7 collective-permute-start.35
  399.5 2.0 fusion.5
  405.5 3.7 collective-permute-done.31
  411.7 2.6 collective-permute-done.32
  (236 shorter events, 79.7 us)
Async XLA Ops:
  7.2 131.2 %all-gather.3.cloned.1.call-start = ((), (), s32[]{:S(2)}) async-start(), calls=%async_computation.2 | async-start | bytes 9732096 | tf_op jit(solution)/shard_map/all_gather | solution.py:604
  10.4 365.9 %reduce-scatter.2.cloned.1.call-start = ((), (), s32[]{:S(2)}) async-start(), calls=%async_computation.1 | async-start | bytes 4734976 | tf_op jit(solution)/shard_map/reduce_scatter | solution.py:663
  10.5 12.3 %collective-permute-start = (bf16[192,384]{1,0:T(8,128)(2,1)S(1)}, bf16[192,384]{1,0:T(8,128)(2,1)S(1)}, u32[]{:S(2)}, u32[]{:S(2)}) collective-permute-start(bf16[192,384]{1,0:T(8,128)(2,1)S(1)} %pad_maximum_fusion.5), channel_id=1, source_target_pairs={{0,8},{2,10},{4,12},{6,14},{8,16},{10,18},{12,20},{14,22},{16,24},... | collective-permute-start | bytes 442376 | tf_op jit(solution)/shard_map/ppermute | solution.py:580
  13.5 12.3 %collective-permute-start.1 = (bf16[192,384]{1,0:T(8,128)(2,1)S(1)}, bf16[192,384]{1,0:T(8,128)(2,1)S(1)}, u32[]{:S(2)}, u32[]{:S(2)}) collective-permute-start(bf16[192,384]{1,0:T(8,128)(2,1)S(1)} %pad_maximum_fusion.5), channel_id=1, source_target_pairs={{0,16},{2,18},{4,20},{6,22},{8,24},{10,26},{12,28},{14,30},{16,0},... | collective-permute-start | bytes 442376 | tf_op jit(solution)/shard_map/ppermute | solution.py:580
  16.1 9.7 %collective-permute-start.2 = (bf16[192,384]{1,0:T(8,128)(2,1)S(1)}, bf16[192,384]{1,0:T(8,128)(2,1)S(1)}, u32[]{:S(2)}, u32[]{:S(2)}) collective-permute-start(bf16[192,384]{1,0:T(8,128)(2,1)S(1)} %pad_maximum_fusion.5), channel_id=1, source_target_pairs={{0,24},{2,26},{4,28},{6,30},{8,0},{10,2},{12,4},{14,6},{16,8},{18,... | collective-permute-start | bytes 442376 | tf_op jit(solution)/shard_map/ppermute | solution.py:580
  17.5 10.0 %collective-permute-start.6 = (bf16[192,384]{1,0:T(8,128)(2,1)S(1)}, bf16[192,384]{1,0:T(8,128)(2,1)S(1)}, u32[]{:S(2)}, u32[]{:S(2)}) collective-permute-start(bf16[192,384]{1,0:T(8,128)(2,1)S(1)} %pad_maximum_fusion.5), channel_id=1, source_target_pairs={{0,4},{2,6},{4,0},{6,2},{8,12},{10,14},{12,8},{14,10},{16,20},{18,... | collective-permute-start | bytes 442376 | tf_op jit(solution)/shard_map/ppermute | solution.py:579
  19.0 27.3 %collective-permute-start.12 = (f32[2816]{0:T(1024)S(1)}, f32[2816]{0:T(1024)S(1)}, u32[]{:S(2)}, u32[]{:S(2)}) collective-permute-start(f32[2816]{0:T(1024)S(1)} %pad_maximum_fusion.7), channel_id=1, source_target_pairs={{0,1},{1,0},{2,3},{3,2},{4,5},{5,4},{6,7},{7,6},{8,9},{9,8},{10,11... | collective-permute-start | bytes 33800 | tf_op jit(solution)/shard_map/ppermute | solution.py:716
  25.9 12.1 %collective-permute-start.7 = (bf16[3,192,384]{2,1,0:T(8,128)(2,1)S(1)}, bf16[3,192,384]{2,1,0:T(8,128)(2,1)S(1)}, u32[]{:S(2)}, u32[]{:S(2)}) collective-permute-start(bf16[3,192,384]{2,1,0:T(8,128)(2,1)S(1)} %pad_maximum_fusion.2), channel_id=1, source_target_pairs={{0,4},{2,6},{4,0},{6,2},{8,12},{10,14},{12,8},{14,10},{16,20},{18,... | collective-permute-start | bytes 1327112 | tf_op jit(solution)/shard_map/ppermute | solution.py:583
  41.3 17.5 %collective-permute-start.9 = (bf16[8,192,384]{2,1,0:T(8,128)(2,1)}, bf16[8,192,384]{2,1,0:T(8,128)(2,1)}, u32[]{:S(2)}, u32[]{:S(2)}) collective-permute-start(bf16[8,192,384]{2,1,0:T(8,128)(2,1)} %bitcast.21.w0.own0), channel_id=1, source_target_pairs={{0,2},{2,0},{4,6},{6,4},{8,10},{10,8},{12,14},{14,12},{16,18},{18,... | collective-permute-start | bytes 3538952 | tf_op jit(solution)/shard_map/ppermute | solution.py:598
  41.3 36.5 %collective-permute-start.8 = (bf16[8,192,384]{2,1,0:T(8,128)(2,1)}, bf16[8,192,384]{2,1,0:T(8,128)(2,1)}, u32[]{:S(2)}, u32[]{:S(2)}) collective-permute-start(bf16[8,192,384]{2,1,0:T(8,128)(2,1)} %bitcast.21.w0.own0), channel_id=1, source_target_pairs={{0,1},{1,0},{2,3},{3,2},{4,5},{5,4},{6,7},{7,6},{8,9},{9,8},{10,11... | collective-permute-start | bytes 3538952 | tf_op jit(solution)/shard_map/ppermute | solution.py:700
  46.9 51.7 %collective-permute-start.13 = (bf16[416,512]{1,0:T(8,128)(2,1)}, bf16[416,512]{1,0:T(8,128)(2,1)}, u32[]{:S(2)}, u32[]{:S(2)}) collective-permute-start(bf16[416,512]{1,0:T(8,128)(2,1)} %pad_maximum_fusion.3), channel_id=1, source_target_pairs={{0,4},{2,6},{4,0},{6,2},{8,12},{10,14},{12,8},{14,10},{16,20},{18,... | collective-permute-start | bytes 1277960 | tf_op jit(solution)/shard_map/ppermute | solution.py:579
  48.5 43.8 %collective-permute-start.3 = (bf16[416,512]{1,0:T(8,128)(2,1)}, bf16[416,512]{1,0:T(8,128)(2,1)}, u32[]{:S(2)}, u32[]{:S(2)}) collective-permute-start(bf16[416,512]{1,0:T(8,128)(2,1)} %pad_maximum_fusion.3), channel_id=1, source_target_pairs={{0,8},{2,10},{4,12},{6,14},{8,16},{10,18},{12,20},{14,22},{16,24},... | collective-permute-start | bytes 1277960 | tf_op jit(solution)/shard_map/ppermute | solution.py:580
  57.5 34.8 %collective-permute-start.4 = (bf16[416,512]{1,0:T(8,128)(2,1)}, bf16[416,512]{1,0:T(8,128)(2,1)S(1)}, u32[]{:S(2)}, u32[]{:S(2)}) collective-permute-start(bf16[416,512]{1,0:T(8,128)(2,1)} %pad_maximum_fusion.3), channel_id=1, source_target_pairs={{0,16},{2,18},{4,20},{6,22},{8,24},{10,26},{12,28},{14,30},{16,0},... | collective-permute-start | bytes 1277960 | tf_op jit(solution)/shard_map/ppermute | solution.py:580
  58.8 37.5 %collective-permute-start.5 = (bf16[416,512]{1,0:T(8,128)(2,1)}, bf16[416,512]{1,0:T(8,128)(2,1)}, u32[]{:S(2)}, u32[]{:S(2)}) collective-permute-start(bf16[416,512]{1,0:T(8,128)(2,1)} %pad_maximum_fusion.3), channel_id=1, source_target_pairs={{0,24},{2,26},{4,28},{6,30},{8,0},{10,2},{12,4},{14,6},{16,8},{18,... | collective-permute-start | bytes 1277960 | tf_op jit(solution)/shard_map/ppermute | solution.py:580
  77.8 22.9 %collective-permute-start.11 = (bf16[8,192,384]{2,1,0:T(8,128)(2,1)}, bf16[8,192,384]{2,1,0:T(8,128)(2,1)}, u32[]{:S(2)}, u32[]{:S(2)}) collective-permute-start(bf16[8,192,384]{2,1,0:T(8,128)(2,1)} %collective-permute-done.8.w0.oth0), channel_id=1, source_target_pairs={{0,2},{2,0},{4,6},{6,4},{8,10},{10,8},{12,14},{14,12},{16,18},{18,... | collective-permute-start | bytes 3538952 | tf_op jit(solution)/shard_map/ppermute | solution.py:598
  98.7 31.9 %collective-permute-start.10 = (bf16[3,416,512]{2,1,0:T(8,128)(2,1)}, bf16[3,416,512]{2,1,0:T(8,128)(2,1)}, u32[]{:S(2)}, u32[]{:S(2)}) collective-permute-start(bf16[3,416,512]{2,1,0:T(8,128)(2,1)} %pad_maximum_fusion), channel_id=1, source_target_pairs={{0,4},{2,6},{4,0},{6,2},{8,12},{10,14},{12,8},{14,10},{16,20},{18,... | collective-permute-start | bytes 3833864 | tf_op jit(solution)/shard_map/ppermute | solution.py:583
  134.8 33.8 %collective-permute-start.15 = (bf16[8,416,512]{2,1,0:T(8,128)(2,1)S(1)}, bf16[8,416,512]{2,1,0:T(8,128)(2,1)}, u32[]{:S(2)}, u32[]{:S(2)}) collective-permute-start(bf16[8,416,512]{2,1,0:T(8,128)(2,1)S(1)} %bitcast.146), channel_id=1, source_target_pairs={{0,2},{2,0},{4,6},{6,4},{8,10},{10,8},{12,14},{14,12},{16,18},{18,... | collective-permute-start | bytes 10223624 | tf_op jit(solution)/shard_map/ppermute | solution.py:598
  136.9 31.0 %collective-permute-start.14 = (bf16[8,128,512]{2,1,0:T(8,128)(2,1)}, bf16[8,128,512]{2,1,0:T(8,128)(2,1)}, u32[]{:S(2)}, u32[]{:S(2)}) collective-permute-start(bf16[8,128,512]{2,1,0:T(8,128)(2,1)} %slice.186), channel_id=1, source_target_pairs={{0,1},{1,0},{2,3},{3,2},{4,5},{5,4},{6,7},{7,6},{8,9},{9,8},{10,11... | collective-permute-start | bytes 3145736 | tf_op jit(solution)/shard_map/ppermute | solution.py:809
  264.0 15.9 %collective-permute-start.18 = (bf16[4,48,1536]{2,1,0:T(8,128)(2,1)}, bf16[4,48,1536]{2,1,0:T(8,128)(2,1)}, u32[]{:S(2)}, u32[]{:S(2)}) collective-permute-start(bf16[4,48,1536]{2,1,0:T(8,128)(2,1)} %dynamic-slice_bitcast_fusion.2), channel_id=1, source_target_pairs={{0,4},{2,6},{4,0},{6,2},{8,12},{10,14},{12,8},{14,10},{16,20},{18,... | collective-permute-start | bytes 1769480 | tf_op jit(solution)/shard_map/ppermute | solution.py:622
  281.2 45.7 %collective-permute-start.23 = (bf16[4,48,1536]{2,1,0:T(8,128)(2,1)S(1)}, bf16[4,48,1536]{2,1,0:T(8,128)(2,1)S(1)}, u32[]{:S(2)}, u32[]{:S(2)}) collective-permute-start(bf16[4,48,1536]{2,1,0:T(8,128)(2,1)S(1)} %dynamic-slice_bitcast_fusion.1), channel_id=1, source_target_pairs={{0,4},{2,6},{4,0},{6,2},{8,12},{10,14},{12,8},{14,10},{16,20},{18,... | collective-permute-start | bytes 1769480 | tf_op jit(solution)/shard_map/ppermute | solution.py:622
  281.8 45.0 %collective-permute-start.20 = (bf16[48,1536]{1,0:T(8,128)(2,1)S(1)}, bf16[48,1536]{1,0:T(8,128)(2,1)S(1)}, u32[]{:S(2)}, u32[]{:S(2)}) collective-permute-start(bf16[48,1536]{1,0:T(8,128)(2,1)S(1)} %get-tuple-element.199), channel_id=1, source_target_pairs={{0,8},{2,10},{4,12},{6,14},{8,16},{10,18},{12,20},{14,22},{16,24},... | collective-permute-start | bytes 442376 | tf_op jit(solution)/shard_map/ppermute | solution.py:629
  301.0 25.8 %collective-permute-start.21 = (bf16[48,1536]{1,0:T(8,128)(2,1)S(1)}, bf16[48,1536]{1,0:T(8,128)(2,1)S(1)}, u32[]{:S(2)}, u32[]{:S(2)}) collective-permute-start(bf16[48,1536]{1,0:T(8,128)(2,1)S(1)} %get-tuple-element.198), channel_id=1, source_target_pairs={{0,16},{2,18},{4,20},{6,22},{8,24},{10,26},{12,28},{14,30},{16,0},... | collective-permute-start | bytes 442376 | tf_op jit(solution)/shard_map/ppermute | solution.py:629
  302.5 24.3 %collective-permute-start.22 = (bf16[48,1536]{1,0:T(8,128)(2,1)S(1)}, bf16[48,1536]{1,0:T(8,128)(2,1)S(1)}, u32[]{:S(2)}, u32[]{:S(2)}) collective-permute-start(bf16[48,1536]{1,0:T(8,128)(2,1)S(1)} %get-tuple-element.197), channel_id=1, source_target_pairs={{0,24},{2,26},{4,28},{6,30},{8,0},{10,2},{12,4},{14,6},{16,8},{18,... | collective-permute-start | bytes 442376 | tf_op jit(solution)/shard_map/ppermute | solution.py:629
  335.6 13.9 %collective-permute-start.24 = (bf16[8,192,384]{2,1,0:T(8,128)(2,1)}, bf16[8,192,384]{2,1,0:T(8,128)(2,1)S(1)}, u32[]{:S(2)}, u32[]{:S(2)}) collective-permute-start(bf16[8,192,384]{2,1,0:T(8,128)(2,1)} %get-tuple-element.159), channel_id=1, source_target_pairs={{0,2},{2,0},{4,6},{6,4},{8,10},{10,8},{12,14},{14,12},{16,18},{18,... | collective-permute-start | bytes 3538952 | tf_op jit(solution)/shard_map/ppermute | solution.py:598
  345.7 31.6 %collective-permute-start.25 = (bf16[48,1536]{1,0:T(8,128)(2,1)}, bf16[48,1536]{1,0:T(8,128)(2,1)}, u32[]{:S(2)}, u32[]{:S(2)}) collective-permute-start(bf16[48,1536]{1,0:T(8,128)(2,1)} %get-tuple-element.196), channel_id=1, source_target_pairs={{0,8},{2,10},{4,12},{6,14},{8,16},{10,18},{12,20},{14,22},{16,24},... | collective-permute-start | bytes 442376 | tf_op jit(solution)/shard_map/ppermute | solution.py:629
  346.8 30.5 %collective-permute-start.26 = (bf16[48,1536]{1,0:T(8,128)(2,1)}, bf16[48,1536]{1,0:T(8,128)(2,1)}, u32[]{:S(2)}, u32[]{:S(2)}) collective-permute-start(bf16[48,1536]{1,0:T(8,128)(2,1)} %get-tuple-element.195), channel_id=1, source_target_pairs={{0,16},{2,18},{4,20},{6,22},{8,24},{10,26},{12,28},{14,30},{16,0},... | collective-permute-start | bytes 442376 | tf_op jit(solution)/shard_map/ppermute | solution.py:629
  348.1 29.2 %collective-permute-start.27 = (bf16[48,1536]{1,0:T(8,128)(2,1)}, bf16[48,1536]{1,0:T(8,128)(2,1)}, u32[]{:S(2)}, u32[]{:S(2)}) collective-permute-start(bf16[48,1536]{1,0:T(8,128)(2,1)} %get-tuple-element.194), channel_id=1, source_target_pairs={{0,24},{2,26},{4,28},{6,30},{8,0},{10,2},{12,4},{14,6},{16,8},{18,... | collective-permute-start | bytes 442376 | tf_op jit(solution)/shard_map/ppermute | solution.py:629
  351.1 26.2 %collective-permute-start.28 = (bf16[4,192,384]{2,1,0:T(8,128)(2,1)S(1)}, bf16[4,192,384]{2,1,0:T(8,128)(2,1)}, u32[]{:S(2)}, u32[]{:S(2)}) collective-permute-start(bf16[4,192,384]{2,1,0:T(8,128)(2,1)S(1)} %dynamic-slice_bitcast_fusion), channel_id=1, source_target_pairs={{0,4},{2,6},{4,0},{6,2},{8,12},{10,14},{12,8},{14,10},{16,20},{18,... | collective-permute-start | bytes 1769480 | tf_op jit(solution)/shard_map/ppermute | solution.py:622
  394.1 16.2 %collective-permute-start.33 = (bf16[192,384]{1,0:T(8,128)(2,1)S(1)}, bf16[192,384]{1,0:T(8,128)(2,1)S(1)}, u32[]{:S(2)}, u32[]{:S(2)}) collective-permute-start(bf16[192,384]{1,0:T(8,128)(2,1)S(1)} %get-tuple-element.191), channel_id=1, source_target_pairs={{0,8},{2,10},{4,12},{6,14},{8,16},{10,18},{12,20},{14,22},{16,24},... | collective-permute-start | bytes 442376 | tf_op jit(solution)/shard_map/ppermute | solution.py:629
  395.0 15.2 %collective-permute-start.34 = (bf16[192,384]{1,0:T(8,128)(2,1)S(1)}, bf16[192,384]{1,0:T(8,128)(2,1)S(1)}, u32[]{:S(2)}, u32[]{:S(2)}) collective-permute-start(bf16[192,384]{1,0:T(8,128)(2,1)S(1)} %get-tuple-element.193), channel_id=1, source_target_pairs={{0,16},{2,18},{4,20},{6,22},{8,24},{10,26},{12,28},{14,30},{16,0},... | collective-permute-start | bytes 442376 | tf_op jit(solution)/shard_map/ppermute | solution.py:629
  396.4 13.9 %collective-permute-start.35 = (bf16[192,384]{1,0:T(8,128)(2,1)S(1)}, bf16[192,384]{1,0:T(8,128)(2,1)S(1)}, u32[]{:S(2)}, u32[]{:S(2)}) collective-permute-start(bf16[192,384]{1,0:T(8,128)(2,1)S(1)} %get-tuple-element.192), channel_id=1, source_target_pairs={{0,24},{2,26},{4,28},{6,30},{8,0},{10,2},{12,4},{14,6},{16,8},{18,... | collective-permute-start | bytes 442376 | tf_op jit(solution)/shard_map/ppermute | solution.py:629
  404.1 13.8 %collective-permute-start.36 = (f32[3,48,512]{2,1,0:T(8,128)S(1)}, f32[3,48,512]{2,1,0:T(8,128)S(1)}, u32[]{:S(2)}, u32[]{:S(2)}) collective-permute-start(f32[3,48,512]{2,1,0:T(8,128)S(1)} %bitcast.159), channel_id=1, source_target_pairs={{0,1},{1,0},{2,3},{3,2},{4,5},{5,4},{6,7},{7,6},{8,9},{9,8},{10,11... | collective-permute-start | bytes 884744 | tf_op jit(solution)/shard_map/ppermute | solution.py:932
  (40 other events, 360.5 us)
Sparse Core Ops, SparseCore 0:
  11.5 111.0 all-gather.2
  264.9 100.4 reduce-scatter.1
